TPU v7x, 128 devices: a whole 4x4x4 slice. The times are simulated.
128 devices in a mesh: dev: 128 (over z, y, x, core).
Axes of the slice: x: 4, y: 4, z: 4, core: 2. Of those that a mesh axis runs over, the one named last changes fastest.
Arguments:
- tokens: bfloat16 [2, 25216, 768], P(None, 'dev'), may hold values from -24 to 24
- cotangent: float32 [2, 25216, 768], P(None, 'dev'), may hold values from -6 to 6
- routes: int32 [2, 25216, 2], P(None, 'dev'), may hold values from 0 to 2, all different within a row; in each aligned block of 197 rows (0 to 196, 197 to 393, ..., all dimensions but the last counted through in order) at most 133 rows name the same one
- qkv_weight: bfloat16 [768, 2304], P('dev'), may hold values from -0.21875 to 0.21875
- out_weight: bfloat16 [768, 768], P('dev'), may hold values from -2 to 2
- norm_gain: bfloat16 [2, 768], P(None, 'dev'), may hold values from 0.5 to 1.5
- bias_rows: bfloat16 [5, 768], P(None, 'dev'), may hold values from -0.59765625 to 0.59765625
- router_weight: bfloat16 [768, 3], P('dev'), may hold values from -0.15625 to 0.15625
- expand_weight: bfloat16 [3, 768, 3072], P(None, 'dev'), may hold values from -0.21875 to 0.21875
- shrink_weight: bfloat16 [3, 3072, 768], P(None, 'dev'), may hold values from -0.21875 to 0.21875
- expert_bias: bfloat16 [3, 3840], P(None, 'dev'), may hold values from -0.59765625 to 0.59765625
- first_qkv: float32 [768, 2304], P('dev'), may hold values from -192 to 192
- first_out: float32 [768, 768], P('dev'), may hold values from -28 to 28
- first_gain: float32 [2, 768], P(None, 'dev'), may hold values from -320 to 320
- first_bias: float32 [5, 768], P(None, 'dev'), may hold values from -256 to 256
- first_router: float32 [768, 3], P('dev'), may hold values from -1536 to 1536
- first_expand: float32 [3, 768, 3072], P(None, 'dev'), may hold values from -40 to 40
- first_shrink: float32 [3, 3072, 768], P(None, 'dev'), may hold values from -40 to 40
- first_expert: float32 [3, 3840], P(None, 'dev'), may hold values from -56 to 56
- second_qkv: float32 [768, 2304], P('dev'), may hold values from 5043.2 to 20172.8
- second_out: float32 [768, 768], P('dev'), may hold values from 84.48 to 332.8
- second_gain: float32 [2, 768], P(None, 'dev'), may hold values from 12608 to 50432
- second_bias: float32 [5, 768], P(None, 'dev'), may hold values from 7564.8 to 30259.2
- second_router: float32 [768, 3], P('dev'), may hold values from 251756.55 to 1007026.2
- second_expand: float32 [3, 768, 3072], P(None, 'dev'), may hold values from 163.904 to 668.224
- second_shrink: float32 [3, 3072, 768], P(None, 'dev'), may hold values from 191.6416 to 756.48
- second_expert: float32 [3, 3840], P(None, 'dev'), may hold values from 327.808 to 1311.232
Outputs:
- output: float32 [2, 25216, 768], P(None, 'dev')
- input_grad: float32 [2, 25216, 768], P(None, 'dev')
- qkv_first: float32 [768, 2304], P('dev')
- qkv_second: float32 [768, 2304], P('dev')
- qkv_new: float32 [768, 2304], P('dev')
- out_first: float32 [768, 768], P('dev')
- out_second: float32 [768, 768], P('dev')
- out_new: float32 [768, 768], P('dev')
- gain_first: float32 [2, 768], P(None, 'dev')
- gain_second: float32 [2, 768], P(None, 'dev')
- gain_new: float32 [2, 768], P(None, 'dev')
- bias_first: float32 [5, 768], P(None, 'dev')
- bias_second: float32 [5, 768], P(None, 'dev')
- bias_new: float32 [5, 768], P(None, 'dev')
- router_first: float32 [768, 3], P('dev')
- router_second: float32 [768, 3], P('dev')
- router_new: float32 [768, 3], P('dev')
- expand_first: float32 [3, 768, 3072], P(None, 'dev')
- expand_second: float32 [3, 768, 3072], P(None, 'dev')
- expand_new: float32 [3, 768, 3072], P(None, 'dev')
- shrink_first: float32 [3, 3072, 768], P(None, 'dev')
- shrink_second: float32 [3, 3072, 768], P(None, 'dev')
- shrink_new: float32 [3, 3072, 768], P(None, 'dev')
- expert_first: float32 [3, 3840], P(None, 'dev')
- expert_second: float32 [3, 3840], P(None, 'dev')
- expert_new: float32 [3, 3840], P(None, 'dev')
Inputs may be any that keep to these rules, and one draw needn't show every extreme that they name: `routes`: each token names 2 different experts. In each aligned block of 197 tokens (one device's tokens of one micro-batch) no expert is named by more than 133 tokens, and in some block one expert is named by exactly 133.
All inputs are finite; a program needn't handle non-finite values.
Results may differ from a plain program's by a relative error of at most 0.015.
Values may be sent and summed in bfloat16 or wider, within the bound.
No kernel may reach another device: no remote copies, remote signals or barrier semaphores. Data moves between devices by JAX's collectives and lax.ppermute only.
A program may use at most 384 MiB of HBM per device.

v0:
```python
import functools

import jax
import jax.numpy as jnp
from jax import lax
from jax.experimental import pallas as pl
from jax.experimental.pallas import tpu as pltpu
from jax.sharding import Mesh
from jax.sharding import PartitionSpec as P

HEAD = 64
SEQ = 197
STEP = 10
CAP = 133
CHIPS = ("dev_0", "dev_1", "dev_2")
CORE = "dev_3"
DEV = ("dev_0", "dev_1", "dev_2", "dev_3")


NORM_EPS = 1e-06
ADAM_EPS = 1e-08
BETA_ONE = 0.9
BETA_TWO = 0.95
ROOT_HALF = 0.7071067811865476
INV_ROOT_TAU = 0.3989422804014327
RATES = (0.04, 0.2, 0.4, 0.04, 0.03, 0.04, 0.05, 0.04)
DECAYS = (0.1, 0.1, 0.0, 0.0, 0.1, 0.1, 0.1, 0.0)


def norm_parts(values):
    average = jnp.mean(values, -1, keepdims=True)
    centred = values - average
    inverse = lax.rsqrt(jnp.mean(centred * centred, -1, keepdims=True) + NORM_EPS)
    return (centred * inverse, inverse)


def norm_back(grad_norm, normed, inverse):
    return inverse * (
        grad_norm
        - jnp.mean(grad_norm, -1, keepdims=True)
        - normed * jnp.mean(grad_norm * normed, -1, keepdims=True)
    )


def softmax_rows(logits):
    shifted = jnp.exp(logits - jnp.max(logits, -1, keepdims=True))
    return shifted / jnp.sum(shifted, -1, keepdims=True)


def swap_cores(x):
    return lax.ppermute(x, CORE, [(0, 1), (1, 0)])


def pad_rows(x, length):
    return jnp.pad(x, [(0, 0)] * (x.ndim - 2) + [(0, length - x.shape[-2]), (0, 0)])


def ring_pairs():
    up = [(2 * i, 2 * ((i + 1) % 4)) for i in range(4)]
    return up + [(2 * i + 1, 2 * ((i - 1) % 4) + 1) for i in range(4)]


def chips_gather(x):
    sign = 1 - 2 * lax.axis_index(CORE)
    moving = lax.all_to_all(jnp.broadcast_to(x, (16, *x.shape)), CHIPS[1:], 0, 0, tiled=True)
    whole = jnp.zeros((4, *moving.shape), x.dtype)
    for step in range(4):
        index = lax.rem(lax.axis_index(CHIPS[0]) - sign * step + 4, 4)
        whole = lax.dynamic_update_index_in_dim(whole, moving, index, 0)
        if step < 3:
            moving = lax.ppermute(moving, (CHIPS[0], CORE), ring_pairs())
    return whole


def round_kernel(sizes, carried, index_ref, *refs):
    outs = refs[len(refs) - carried - len(sizes) : len(refs) - carried]
    at = 0
    for size, out_ref in zip(sizes, outs):
        total = sum([refs[at + k][...].astype(jnp.float32) for k in range(size)])
        out_ref[...] = total.astype(jnp.bfloat16)
        at += size


class Ring:
    def __init__(self, terms, *axes):
        self.shape = terms[0].shape[1:]
        self.terms = [a.reshape(4, 4, 4, *self.shape) for a in terms]
        self.names, self.axes = list(CHIPS), [CHIPS[k] for k in axes]
        self.step, self.piece = 0, None

    def place(self):
        return self.names.index(self.axes[0])

    def pass_on(self):
        return lax.ppermute(self.piece, (self.axes[0], CORE), ring_pairs())

    def advance(self, piece):
        self.step, self.piece = self.step + 1, piece
        if self.step == 4:
            self.names.remove(self.axes.pop(0))
            self.step, self.terms = 0, [piece]

    def total(self):
        return totals([self])[0]


def totals(rings):
    blocks = jnp.concatenate([r.piece.reshape(-1, *r.shape) for r in rings], 1)
    blocks = lax.all_to_all(blocks, tuple(rings[0].names), 0, 0, tiled=True)
    return jnp.split(jnp.sum(blocks.astype(jnp.float32), 0), len(rings))


def next_round(rings, after=(), carry=()):
    sign = 1 - 2 * lax.axis_index(CORE)
    index, arrays, specs, sizes = [], [], [], []
    outs = []
    for n, ring in enumerate(rings):
        index.append(lax.rem(lax.axis_index(ring.axes[0]) - sign * (1 + ring.step) + 8, 4))
        others = (1, 4)[: len(ring.names) - 1]
        block, place = list(others), ring.place()
        block.insert(place, None)
        tail = (0,) * (len(ring.shape) + len(others) - 1)

        def where(g, index_ref, place=place, n=n, tail=tail):
            at = [g, *tail]
            at.insert(place, index_ref[n])
            return tuple(at)

        moved = pl.BlockSpec((*others, *ring.shape), lambda g, _, tail=tail: (g, *tail))
        arrays += ring.terms
        specs += [pl.BlockSpec((*block, *ring.shape), where)] * len(ring.terms)
        sizes.append(len(ring.terms) + (1 if ring.step else 0))
        if ring.step:
            arrays.append(ring.pass_on())
            specs.append(moved)
        shape = (*(4,) * len(others), *ring.shape)
        outs.append((jax.ShapeDtypeStruct(shape, jnp.bfloat16), moved))
    at = 1 + len(arrays) + len(after)
    *pieces, = pl.pallas_call(
        functools.partial(round_kernel, sizes, len(carry)),
        grid_spec=pltpu.PrefetchScalarGridSpec(
            num_scalar_prefetch=1,
            grid=(4,),
            in_specs=specs + [pl.BlockSpec(memory_space=pl.ANY)] * (len(after) + len(carry)),
            out_specs=[spec for _, spec in outs]
            + [pl.BlockSpec(memory_space=pl.ANY)] * len(carry),
        ),
        out_shape=[shape for shape, _ in outs]
        + [jax.ShapeDtypeStruct(a.shape, a.dtype) for a in carry],
        input_output_aliases={at + k: len(outs) + k for k in range(len(carry))},
        compiler_params=pltpu.CompilerParams(vmem_limit_bytes=58 * 1024 * 1024),
        cost_estimate=pl.CostEstimate(
            flops=0, bytes_accessed=5_500_000 * len(rings), transcendentals=0
        ),
    )(jnp.stack(index).astype(jnp.int32), *arrays, *after, *carry)
    for ring, piece in zip(rings, pieces):
        ring.advance(piece)
    return tuple(pieces)


def gelu_both(z):
    half = 0.5 * (1.0 + lax.erf(z * ROOT_HALF))
    return z * half, half + z * jnp.exp(-0.5 * z * z) * INV_ROOT_TAU


SLOTS = 272


def mm(a, b, dims):
    return lax.dot_general(a, b, (dims, ((), ())), preferred_element_type=jnp.float32)


def two_terms(x):
    high = x.astype(jnp.bfloat16)
    return high, (x - high.astype(jnp.float32)).astype(jnp.bfloat16)


def to_wide(core, mine, other):
    mine, other = mine.astype(jnp.float32), other.astype(jnp.float32)
    both = jnp.stack([jnp.where(core == 0, mine, other), jnp.where(core == 0, other, mine)], 1)
    return both.reshape(1024, both.shape[-1]).astype(jnp.bfloat16)


def by_core(core, x, own_ref, send_ref):
    parts = x.reshape(own_ref.shape[0], 2, *own_ref.shape[1:])
    own_ref[...] = jnp.where(core == 0, parts[:, 0], parts[:, 1]).astype(jnp.bfloat16)
    send_ref[...] = jnp.where(core == 0, parts[:, 1], parts[:, 0]).astype(jnp.bfloat16)


def spread_out(x, spread):
    return mm(x, spread, ((1,), (0,))).astype(jnp.bfloat16)


def pull_in(x, spread):
    high, low = two_terms(x)
    return mm(high, spread, ((1,), (1,))) + mm(low, spread, ((1,), (1,)))


def ones_where(mask):
    return mask.astype(jnp.float32).astype(jnp.bfloat16)


def biases_of_devices():
    device = lax.broadcasted_iota(jnp.int32, (128, 3840), 0)
    value = lax.broadcasted_iota(jnp.int32, (128, 3840), 1)
    return (value >= 30 * device) & (value < 30 * device + 30)


def spare_rows():
    place = lax.broadcasted_iota(jnp.int32, (1024, 128), 0)
    return ones_where(place == 8 * lax.broadcasted_iota(jnp.int32, (1024, 128), 1) + 6)


def qkv_kernel(
    core_ref, mine_ref, other_ref, small_mine_ref, small_other_ref, spread_ref, tokens_ref,
    of_device_ref, qkv_ref, wide_ref, small_ref, ebias_ref,
):
    j = pl.program_id(0)
    core = core_ref[0]

    @pl.when(j == 0)
    def _():
        small = to_wide(core, small_mine_ref[...], small_other_ref[...])
        small_ref[...] = mm(small, spread_ref[...], ((0,), (1,)))
        blocks = mm(spare_rows(), small, ((0,), (0,))).astype(jnp.bfloat16)
        for e in range(3):
            spaced = mm(blocks[:, 32 * e : 32 * e + 32], of_device_ref[:, :32], ((1,), (1,)))
            ebias_ref[e] = jnp.sum(jnp.where(biases_of_devices(), spaced, 0.0), 0, keepdims=True)
        for b in range(2):
            normed, _ = norm_parts(tokens_ref[b].astype(jnp.float32))
            rows = (normed * small_ref[0:1] + small_ref[2:3]).astype(jnp.bfloat16)
            wide_ref[b] = spread_out(rows, spread_ref[...])

    weight = to_wide(core, mine_ref[...], other_ref[...])
    bias = jnp.where(j == 0, small_ref[4:5], jnp.where(j == 1, 0.0, small_ref[5:6]))
    for b in range(2):
        qkv_ref[b] = (mm(wide_ref[b], weight, ((1,), (0,))) + bias).astype(jnp.bfloat16)


def head_probs(query, key):
    scores = mm(query, key, ((1,), (1,))) * (HEAD ** (-0.5))
    return softmax_rows(scores)


def attend_kernel(
    core_ref, mine_ref, other_ref, qkv_ref, tokens_ref, routes_ref, small_ref, spread_ref,
    attended_ref, middle_ref, input_ref, prob_ref, gate_ref, kept,
):
    core = core_ref[0]
    width = tokens_ref.shape[-1]
    for pair in range(width // (2 * HEAD)):
        parts = []
        for h in (2 * pair, 2 * pair + 1):
            query, key, value = [
                qkv_ref[:, k * width + h * HEAD : k * width + (h + 1) * HEAD] for k in range(3)
            ]
            weights = head_probs(query, key).astype(jnp.bfloat16)
            parts.append(mm(weights, value, ((1,), (0,))))
        kept[:, pair * 128 : pair * 128 + 128] = jnp.concatenate(parts, 1).astype(jnp.bfloat16)
    spread = spread_ref[...]
    attended = spread_out(kept[...], spread)
    attended_ref[...] = attended
    weight = to_wide(core, mine_ref[...], other_ref[...])
    branch = mm(attended, weight, ((1,), (0,))) + small_ref[6:7]
    middle = tokens_ref[...].astype(jnp.float32) + branch
    middle_ref[...] = middle
    normed, _ = norm_parts(middle)
    rows = (normed * small_ref[1:2] + small_ref[3:4]).astype(jnp.bfloat16)
    input_ref[...] = spread_out(rows, spread)
    logits = mm(rows, small_ref[7:10].astype(jnp.bfloat16), ((1,), (1,)))
    prob = softmax_rows(logits)
    prob_ref[...] = prob
    experts = lax.broadcasted_iota(jnp.int32, prob.shape, 1)
    routes = routes_ref[...]
    member = ((experts == routes[:, 0:1]) | (experts == routes[:, 1:2])).astype(jnp.float32)
    chosen = member * prob
    gate_ref[...] = chosen / jnp.sum(chosen, 1, keepdims=True)


def expert_kernel(
    e, core_ref, w2_ref, w1_ref, b1_ref, b2_ref, x_ref, cot_ref, slot_row_ref, slot_col_ref,
    gate_ref, out_in_ref, *rest,
):
    (
        own_ref, send_ref, db1_ref, db2_ref, out_ref, dx_ref, gg_ref,
        xs, xts, rs, rows_acc, dx_acc, kept, sems,
    ) = rest[-14:]
    dx_in_ref = rest[0] if e > 0 else None
    i = pl.program_id(0)
    core = core_ref[0]
    tokens = x_ref.shape[1]

    @pl.when(i == 0)
    def _():
        taken, grads = 0.0, 0.0
        for b in range(2):
            slots = lax.broadcasted_iota(jnp.int32, (SLOTS, tokens), 0)
            pick = ones_where(slots == slot_row_ref[b, e : e + 1, :])
            taken += mm(pick, x_ref[b], ((1,), (0,)))
            scaled = (gate_ref[b][:, e : e + 1] * cot_ref[b]).astype(jnp.bfloat16)
            grads += mm(pick, scaled, ((1,), (0,)))
        xs[...] = taken.astype(jnp.bfloat16)
        xts[...] = taken.T.astype(jnp.bfloat16)
        rs[...] = grads.astype(jnp.bfloat16)
        db2_ref[...] = jnp.sum(grads, 0, keepdims=True)
        rows_acc[...] = jnp.zeros_like(rows_acc) + b2_ref[...]
        dx_acc[...] = jnp.zeros_like(dx_acc)

    x = xs[...]
    r = rs[...]
    w1 = w1_ref[...].astype(jnp.float32).reshape(1024, 768).astype(jnp.bfloat16)
    w2 = w2_ref[...].astype(jnp.float32).reshape(768, 768).astype(jnp.bfloat16)
    hidden = mm(x, w1, ((1,), (0,))) + b1_ref[...]
    act, slope = gelu_both(hidden)
    act = act.astype(jnp.bfloat16)
    rows_acc[...] += mm(act, w2, ((1,), (0,)))
    dw2 = mm(act, r, ((0,), (0,))).reshape(16, 2, 3, 8, 768)
    for c in range(2):
        kept[c, pl.ds(pl.multiple_of(16 * i, 16), 16), 4:7] = dw2[:, c].astype(jnp.bfloat16)
    dh = mm(r, w2, ((1,), (1,))) * slope
    dh = dh.astype(jnp.bfloat16)
    db1_ref[...] = jnp.sum(dh.astype(jnp.float32), 0, keepdims=True)
    dw1 = mm(xts[...], dh, ((1,), (0,))).reshape(64, 2, 1, 8, 768)
    for c in range(2):
        kept[c, :, pl.ds(i, 1)] = dw1[:, c].astype(jnp.bfloat16)
    dx_acc[...] += mm(dh, w1, ((1,), (1,)))

    def copies(step):
        parts = [
            (slice(None), pl.ds(step, 1)),
            (pl.ds(pl.multiple_of(16 * step, 16), 16), pl.ds(4, 3)),
        ]
        pairs = [(kept.at[core], own_ref), (kept.at[1 - core], send_ref)]
        return [
            pltpu.make_async_copy(source.at[part], ref.at[part], sems.at[step, 2 * k + m])
            for k, (source, ref) in enumerate(pairs)
            for m, part in enumerate(parts)
        ]

    for copy in copies(i):
        copy.start()

    @pl.when(i == pl.num_programs(0) - 1)
    def _():
        rows_terms = two_terms(rows_acc[...])
        dx_terms = two_terms(dx_acc[...])
        for b in range(2):
            slots = lax.broadcasted_iota(jnp.int32, (tokens, SLOTS), 1)
            put = ones_where(slots == slot_col_ref[b][:, e : e + 1])
            rows = sum([mm(put, term, ((1,), (0,))) for term in rows_terms])
            out_ref[b] = out_in_ref[b] + gate_ref[b][:, e : e + 1] * rows
            gg_ref[b] = jnp.sum(rows * cot_ref[b], 1, keepdims=True)
            grad = sum([mm(put, term, ((1,), (0,))) for term in dx_terms])
            dx_ref[b] = grad if e == 0 else dx_in_ref[b] + grad
        for step in range(4):
            for copy in copies(step):
                copy.wait()


def route_back_kernel(
    core_ref, mine_ref, other_ref, dx_ref, gg0_ref, gg1_ref, gg2_ref, prob_ref, gate_ref,
    slots_ref, middle_ref, cot_ref, attended_ref, small_ref, spread_ref, *rest,
):
    grad_ref, attended_grad_ref, own_ref, send_ref, small_out_ref = rest[-5:]
    core = core_ref[0]
    spread = spread_ref[...]
    weight = to_wide(core, mine_ref[...], other_ref[...])
    router = small_ref[7:10].astype(jnp.bfloat16)
    total, sums, router_grad = 0.0, [0.0, 0.0, 0.0], 0.0
    for b in range(2):
        prob, gate = prob_ref[b], gate_ref[b]
        experts = lax.broadcasted_iota(jnp.int32, prob.shape, 1)
        gate_grad = jnp.where(
            experts == 0, gg0_ref[b], jnp.where(experts == 1, gg1_ref[b], gg2_ref[b])
        )
        member = (slots_ref[b] >= 0).astype(jnp.float32)
        chosen = jnp.sum(member * prob, 1, keepdims=True)
        share = jnp.sum(gate_grad * gate, 1, keepdims=True)
        prob_grad = member * (gate_grad - share) / chosen
        logit_grad = prob * (prob_grad - jnp.sum(prob * prob_grad, 1, keepdims=True))
        logit_grad = logit_grad.astype(jnp.bfloat16)
        normed, inverse = norm_parts(middle_ref[b])
        rows = (normed * small_ref[1:2] + small_ref[3:4]).astype(jnp.bfloat16)
        router_grad += mm(logit_grad, rows, ((0,), (0,)))
        grad = pull_in(dx_ref[b], spread) + mm(logit_grad, router, ((1,), (0,)))
        sums[0] += jnp.sum(grad * normed, 0, keepdims=True)
        sums[1] += jnp.sum(grad, 0, keepdims=True)
        grad = cot_ref[b] + norm_back(grad * small_ref[1:2], normed, inverse)
        grad_ref[b] = grad
        branch = grad.astype(jnp.bfloat16)
        sums[2] += jnp.sum(branch.astype(jnp.float32), 0, keepdims=True)
        total += mm(attended_ref[b], branch, ((0,), (0,)))
        wide = mm(branch, weight, ((1,), (1,))).astype(jnp.bfloat16)
        attended_grad_ref[b] = mm(wide, spread, ((1,), (1,))).astype(jnp.bfloat16)
    by_core(core, total, own_ref, send_ref)
    for k in range(3):
        small_out_ref[k : k + 1] = sums[k]
    small_out_ref[3:6] = router_grad


def attend_back_kernel(qkv_ref, grad_ref, *rest):
    out_ref = rest[-1]
    width = grad_ref.shape[-1]
    scaling = HEAD ** (-0.5)
    for pair in range(width // (2 * HEAD)):
        parts = [[], [], []]
        for h in (2 * pair, 2 * pair + 1):
            query, key, value = [
                qkv_ref[:, k * width + h * HEAD : k * width + (h + 1) * HEAD] for k in range(3)
            ]
            grad = grad_ref[:, h * HEAD : (h + 1) * HEAD]
            probs = head_probs(query, key)
            prob_grad = mm(grad, value, ((1,), (1,)))
            score_grad = probs * (prob_grad - jnp.sum(probs * prob_grad, 1, keepdims=True))
            score_grad = score_grad.astype(jnp.bfloat16)
            parts[0].append(mm(score_grad, key, ((1,), (0,))) * scaling)
            parts[1].append(mm(score_grad, query, ((0,), (0,))) * scaling)
            parts[2].append(mm(probs.astype(jnp.bfloat16), grad, ((0,), (0,))))
        for k in range(3):
            at = k * width + pair * 128
            out_ref[:, at : at + 128] = jnp.concatenate(parts[k], 1).astype(jnp.bfloat16)


def qkv_back_kernel(
    core_ref, mine_ref, other_ref, qkv_grad0_ref, qkv_grad1_ref, wide_ref, tokens_ref, grad_ref,
    small_ref, early_ref, in0_ref, in1_ref, in2_ref, out0_ref, out1_ref, out2_ref, of_device_ref,
    spread_ref, *rest,
):
    own_ref, send_ref, small_own_ref, small_send_ref, input_grad_ref, acc, sums = rest[-7:]
    j = pl.program_id(0)
    core = core_ref[0]
    weight = to_wide(core, mine_ref[...], other_ref[...])

    @pl.when(j == 0)
    def _():
        acc[...] = jnp.zeros_like(acc)
        sums[...] = jnp.zeros_like(sums)
        sums[1:2] = early_ref[0:1]
        sums[3:4] = early_ref[1:2]
        sums[6:10] = early_ref[2:6]

    total, bias = 0.0, 0.0
    for b in range(2):
        grad = (qkv_grad0_ref, qkv_grad1_ref)[b][...]
        total += mm(wide_ref[b], grad, ((0,), (0,)))
        bias += jnp.sum(grad.astype(jnp.float32), 0, keepdims=True)
        acc[b] += mm(grad, weight, ((1,), (1,)))
    by_core(core, total, own_ref, send_ref)

    @pl.when(j == 0)
    def _():
        sums[4:5] += bias

    @pl.when(j == 2)
    def _():
        sums[5:6] += bias
        spread = spread_ref[...]
        for b in range(2):
            normed, inverse = norm_parts(tokens_ref[b].astype(jnp.float32))
            grad = pull_in(acc[b], spread)
            sums[0:1] += jnp.sum(grad * normed, 0, keepdims=True)
            sums[2:3] += jnp.sum(grad, 0, keepdims=True)
            input_grad_ref[b] = grad_ref[b] + norm_back(grad * small_ref[0:1], normed, inverse)
        small = mm(spread, sums[...].astype(jnp.bfloat16), ((0,), (1,)))
        blocks = []
        for inner, outer in ((in0_ref, out0_ref), (in1_ref, out1_ref), (in2_ref, out2_ref)):
            biases = jnp.concatenate([inner[...], outer[...]], 1)
            spaced = jnp.where(biases_of_devices(), biases, 0.0).astype(jnp.bfloat16)
            blocks.append(mm(spaced, of_device_ref[...], ((1,), (0,)))[:, :32])
        blocks.append(jnp.zeros((128, 32), jnp.float32))
        blocks = jnp.concatenate(blocks, 1).astype(jnp.bfloat16)
        small += mm(spare_rows(), blocks, ((1,), (0,)))
        by_core(core, small, small_own_ref, small_send_ref)


def pair_kernel(own_qkv, got_qkv, own_out, got_out, own_small, got_small, *rest):
    out_ref = rest[-1]
    at = 0
    for own, got in ((own_qkv, got_qkv), (own_out, got_out), (own_small, got_small)):
        total = own[...].astype(jnp.float32) + got[...].astype(jnp.float32)
        out_ref[:, :, at : at + own.shape[2]] = total.astype(jnp.bfloat16)
        at += own.shape[2]


def call(kernel, grid, ins, outs, scratch=(), after=(), flops=0):
    def spec(shape, block, index):
        if block == "any":
            return pl.BlockSpec(memory_space=pl.ANY)
        if block is None:
            return pl.BlockSpec(shape, lambda *_: (0,) * len(shape))
        return pl.BlockSpec(block, index)

    in_specs = [
        pl.BlockSpec(memory_space=pltpu.SMEM)
        if block == "smem"
        else spec(array.shape, block, index)
        for array, block, index in ins
    ]
    in_specs += [pl.BlockSpec(memory_space=pl.ANY)] * len(after)
    arrays = [array for array, _, _ in ins]
    return pl.pallas_call(
        kernel,
        grid=grid,
        in_specs=in_specs,
        out_specs=[spec(shape, block, index) for shape, _, block, index in outs],
        out_shape=[jax.ShapeDtypeStruct(shape, kind) for shape, kind, _, _ in outs],
        scratch_shapes=list(scratch),
        compiler_params=pltpu.CompilerParams(vmem_limit_bytes=58 * 1024 * 1024),
        cost_estimate=pl.CostEstimate(flops=flops, bytes_accessed=2_000_000_000, transcendentals=0),
    )(*arrays, *after)


def adam_update(weight, gradient, first_old, second_old, rate_value, decay_rate):
    first_new = BETA_ONE * first_old + (1.0 - BETA_ONE) * gradient
    second_new = BETA_TWO * second_old + (1.0 - BETA_TWO) * gradient * gradient
    weight_full = weight.astype(jnp.float32)
    ratio = (
        first_new
        / (1.0 - BETA_ONE**STEP)
        / (jnp.sqrt(second_new / (1.0 - BETA_TWO**STEP)) + ADAM_EPS)
    )
    return (first_new, second_new, weight_full - rate_value * (ratio + decay_rate * weight_full))


def on_device(
    tokens,
    cotangent,
    routes,
    qkv_weight,
    out_weight,
    norm_gain,
    bias_rows,
    router_weight,
    expand_weight,
    shrink_weight,
    expert_bias,
    *moments,
):
    f32, bf = jnp.float32, jnp.bfloat16
    core = lax.axis_index(CORE)
    core_word = (core.astype(jnp.int32).reshape(1), "smem", None)
    micro, rows, width = tokens.shape

    def all_of(array):
        return (array, None, None)

    attn_own = jnp.concatenate(
        [qkv_weight, out_weight, norm_gain.T, bias_rows.T, router_weight, jnp.zeros((6, 118), bf)], 1
    )
    ebias_own = jnp.pad(expert_bias, [(0, 0), (0, 2)]).reshape(1, 96)
    attn_own = jnp.concatenate(
        [attn_own, jnp.pad(ebias_own, [(0, 1), (3072, 32)])], 0
    )
    mine = chips_gather(attn_own).reshape(64, 8, 3200)
    other = swap_cores(mine)

    w1_own = pad_rows(expand_weight, 8).reshape(3, 8, 4, 768).transpose(0, 2, 1, 3)
    expert_own = jnp.concatenate([shrink_weight.reshape(3, 3, 8, 768), w1_own], 1)
    expert_whole = lax.all_gather(expert_own[None], DEV, axis=0, tiled=True)

    def column(array, k, n=768):
        return (array, (64, 8, n), lambda *_: (0, 0, k))

    def columns(array):
        return (array, (64, 8, 768), lambda j: (0, 0, j))

    hot = (routes[:, :, :, None] == jnp.arange(3, dtype=jnp.int32)).astype(f32)
    member = jnp.sum(hot, 2).reshape(micro * rows, 3)
    lower = jnp.arange(micro * rows)[:, None] >= jnp.arange(micro * rows)[None, :]
    position = jnp.dot(lower.astype(bf), member.astype(bf), preferred_element_type=f32) - 1.0
    slots = jnp.where(member > 0, position, -1.0).astype(jnp.int32).reshape(micro, rows, 3)
    slot_rows = slots.transpose(0, 2, 1)

    spread = (
        (jnp.arange(width) // 6 * 8 + jnp.arange(width) % 6)[:, None] == jnp.arange(1024)[None, :]
    ).astype(bf)

    of_device = (jnp.arange(3840)[:, None] % 30 == jnp.arange(128)[None, :]).astype(bf)

    qkv, attn_wide, small, ebias = call(
        qkv_kernel,
        (3,),
        [
            core_word, columns(mine), columns(other), column(mine, 24, 128),
            column(other, 24, 128), all_of(spread), all_of(tokens), all_of(of_device),
        ],
        [
            ((micro, rows, 3 * width), bf, (micro, rows, 768), lambda j: (0, 0, j)),
            ((micro, rows, 1024), bf, None, None),
            ((128, width), f32, None, None),
            ((3, 1, 3840), f32, None, None),
        ],
        flops=2 * 394 * 1024 * 3000,
    )

    def one(array):
        return (array, (None, *array.shape[1:]), lambda b: (b, 0, 0))

    def one_out(n, kind):
        return ((micro, rows, n), kind, (None, rows, n), lambda b: (b, 0, 0))

    attended, middle, expert_input, prob, gates = call(
        attend_kernel,
        (micro,),
        [
            core_word, column(mine, 3), column(other, 3), one(qkv), one(tokens), one(routes),
            all_of(small), all_of(spread),
        ],
        [
            one_out(1024, bf), one_out(width, f32), one_out(1024, bf), one_out(3, f32),
            one_out(3, f32),
        ],
        [pltpu.VMEM((rows, width), bf)],
        flops=2 * 394 * 1024 * 2400,
    )

    output = middle
    wide_grad = None
    gate_grads, inner, outer, rings = [], [], [], []

    follow = ()
    for e in range(3):
        own, send, db1, db2, output, wide_grad, gg = call(
            functools.partial(expert_kernel, e),
            (4,),
            [
                core_word,
                (expert_whole, (32, None, 3, 8, 768), lambda i, e=e: (i, e, 0, 0, 0)),
                (expert_whole, (128, None, 1, 8, 768), lambda i, e=e: (0, e, 3 + i, 0, 0)),
                (ebias, (None, 1, 768), lambda i, e=e: (e, 0, i)),
                (ebias, (None, 1, 768), lambda i, e=e: (e, 0, 4)),
                all_of(expert_input), all_of(cotangent), all_of(slot_rows), all_of(slots),
                all_of(gates), all_of(output),
            ]
            + ([all_of(wide_grad)] if e else []),
            [
                ((64, 7, 8, 768), bf, "any", None),
                ((64, 7, 8, 768), bf, "any", None),
                ((1, 3072), f32, (1, 768), lambda i: (0, i)),
                ((1, 768), f32, None, None),
                ((micro, rows, width), f32, None, None),
                ((micro, rows, 1024), f32, None, None),
                ((micro, rows, 1), f32, None, None),
            ],
            [
                pltpu.VMEM((SLOTS, 1024), bf),
                pltpu.VMEM((1024, SLOTS), bf),
                pltpu.VMEM((SLOTS, 768), bf),
                pltpu.VMEM((SLOTS, 768), f32),
                pltpu.VMEM((SLOTS, 1024), f32),
                pltpu.VMEM((2, 64, 7, 8, 768), bf),
                pltpu.SemaphoreType.DMA((4, 4)),
            ],
            after=follow,
            flops=6 * 2 * SLOTS * 900 * 3072,
        )
        gate_grads.append(gg)
        inner.append(db1)
        outer.append(db2)
        if e == 1:
            *follow, send = next_round(rings, (gg,), (send,))
        elif e == 2:
            *follow, send = next_round(rings, (gg,), (send,))
        rings.append(Ring((own, swap_cores(send)), *((0, 1), (1, 2), (2, 1))[e]))

    middle_grad, attended_grad, own_out, send_out, small_grad = call(
        route_back_kernel,
        (1,),
        [
            core_word, column(mine, 3), column(other, 3), all_of(wide_grad),
            all_of(gate_grads[0]), all_of(gate_grads[1]), all_of(gate_grads[2]), all_of(prob),
            all_of(gates), all_of(slots), all_of(middle), all_of(cotangent), all_of(attended),
            all_of(small),
            all_of(spread),
        ],
        [
            ((micro, rows, width), f32, None, None),
            ((micro, rows, width), bf, None, None),
            ((64, 8, 768), bf, None, None),
            ((64, 8, 768), bf, None, None),
            ((8, width), f32, None, None),
        ],
        after=follow,
        flops=2 * 394 * 1024 * 4000,
    )
    qkv_grads = []
    follow = next_round(rings, (small_grad,))
    for b in range(micro):
        qkv_grads.append(
            call(
                attend_back_kernel,
                (1,),
                [
                    (qkv, (None, rows, 3 * width), lambda _, b=b: (b, 0, 0)),
                    (attended_grad, (None, rows, width), lambda _, b=b: (b, 0, 0)),
                ],
                [((rows, 3 * width), bf, None, None)],
                after=qkv_grads if b else follow,
                flops=2 * 197 * 1024 * 4000,
            )[0]
        )
    next_round(rings, qkv_grads[1:])
    follow = next_round(rings[:1])
    own_qkv, send_qkv, own_small, send_small, input_grad = call(
        qkv_back_kernel,
        (3,),
        [
            core_word, columns(mine), columns(other),
            *[(grad, (rows, 768), lambda j: (0, j)) for grad in qkv_grads],
            all_of(attn_wide), all_of(tokens), all_of(middle_grad), all_of(small),
            all_of(small_grad), *[all_of(a) for a in inner], *[all_of(a) for a in outer],
            all_of(of_device), all_of(spread),
        ],
        [
            ((64, 8, 3 * width), bf, (64, 8, 768), lambda j: (0, 0, j)),
            ((64, 8, 3 * width), bf, (64, 8, 768), lambda j: (0, 0, j)),
            ((64, 8, 128), bf, None, None),
            ((64, 8, 128), bf, None, None),
            ((micro, rows, width), f32, None, None),
        ],
        [pltpu.VMEM((micro, rows, 1024), f32), pltpu.VMEM((128, width), f32)],
        after=follow,
        flops=2 * 394 * 1024 * 5000,
    )

    follow = next_round(rings[1:], (own_small,))
    def chips_part(n):
        return (16, 8, n), lambda i: (i, 0, 0)

    parts = ((own_qkv, send_qkv), (own_out, send_out), (own_small, send_small))
    pair = call(
        pair_kernel,
        (4,),
        [
            (a, *chips_part(own.shape[2])) for own, send in parts for a in (own, swap_cores(send))
        ],
        [((64, 8, 3200), bf, *chips_part(3200))],
        after=follow,
    )[0]
    attn_ring = Ring((pair,), 0)
    for _ in range(3):
        next_round(rings, next_round([attn_ring]))
    next_round([attn_ring])
    attn_sum = attn_ring.total()
    next_round(rings[1:], (attn_ring.piece,))
    next_round(rings[2:], (attn_sum,))
    expert_sums = [rings[0].total(), *totals(rings[1:])]
    ebias_sum = attn_sum[6, 3072:3168].reshape(3, 32)[:, :30]
    attn_sum = attn_sum[:6]
    small_sum = attn_sum[:, 3072:]
    gain_sum, shift_sum, router_sum = small_sum[:, :2].T, small_sum[:, 2:7].T, small_sum[:, 7:10]
    expert_sums = jnp.stack(expert_sums)
    expand_sum = expert_sums[:, :4, :6].transpose(0, 2, 1, 3).reshape(3, 6, 3072)
    shrink_sum = expert_sums[:, 4:].reshape(3, 24, 768)

    weights_all = (
        qkv_weight,
        out_weight,
        norm_gain,
        bias_rows,
        router_weight,
        expand_weight,
        shrink_weight,
        expert_bias,
    )
    grads_all = (
        attn_sum[:, :2304],
        attn_sum[:, 2304:3072],
        gain_sum,
        shift_sum,
        router_sum,
        expand_sum,
        shrink_sum,
        ebias_sum,
    )
    results = [output, input_grad]
    for k in range(8):
        results.extend(
            adam_update(
                weights_all[k], grads_all[k], moments[k], moments[8 + k], RATES[k], DECAYS[k]
            )
        )
    return tuple(results)


def solution(mesh):
    split = Mesh(mesh.devices.reshape(4, 4, 4, 2), ("dev_0", "dev_1", "dev_2", "dev_3"))
    placed = (
        P(None, DEV, None),
        P(None, DEV, None),
        P(None, DEV, None),
        P(DEV, None),
        P(DEV, None),
        P(None, DEV),
        P(None, DEV),
        P(DEV, None),
        P(None, DEV, None),
        P(None, DEV, None),
        P(None, DEV),
        P(DEV, None),
        P(DEV, None),
        P(None, DEV),
        P(None, DEV),
        P(DEV, None),
        P(None, DEV, None),
        P(None, DEV, None),
        P(None, DEV),
        P(DEV, None),
        P(DEV, None),
        P(None, DEV),
        P(None, DEV),
        P(DEV, None),
        P(None, DEV, None),
        P(None, DEV, None),
        P(None, DEV),
    )
    return jax.shard_map(
        on_device,
        mesh=split,
        in_specs=placed,
        out_specs=(
            P(None, DEV, None),
            P(None, DEV, None),
            P(DEV, None),
            P(DEV, None),
            P(DEV, None),
            P(DEV, None),
            P(DEV, None),
            P(DEV, None),
            P(None, DEV),
            P(None, DEV),
            P(None, DEV),
            P(None, DEV),
            P(None, DEV),
            P(None, DEV),
            P(DEV, None),
            P(DEV, None),
            P(DEV, None),
            P(None, DEV, None),
            P(None, DEV, None),
            P(None, DEV, None),
            P(None, DEV, None),
            P(None, DEV, None),
            P(None, DEV, None),
            P(None, DEV),
            P(None, DEV),
            P(None, DEV),
        ),
        check_vma=False,
    )
```

profile of v0, /device:TPU:0, one launch (start us, length us, event | category | flops | bytes accessed | tf_op | source)
XLA Modules:
  0.0 467.7 jit_solution(1675277302019281342)
XLA Ops:
  14.8 7.2 %all-to-all-start = ((bf16[16,8,3200]{2,1,0:T(8,128)(2,1)}), bf16[16,8,3200]{2,1,0:T(8,128)(2,1)}, u32[]{:S(2)}, u32[]{:S(2)}) async-start(bf16[16,8,3200]{2,1,0:T(8,128)(2,1)} %broadcast_in_dim.38), calls=%async_computation | async-start | bytes 1638400 | tf_op jit(solution)/shard_map/all_to_all | solution.py:65
  22.0 16.3 %all-to-all-done = bf16[16,8,3200]{2,1,0:T(8,128)(2,1)} async-done(((bf16[16,8,3200]{2,1,0:T(8,128)(2,1)}), bf16[16,8,3200]{2,1,0:T(8,128)(2,1)}, u32[]{:S(2)}, u32[]{:S(2)}) %all-to-all-start) | async-done | bytes 819232 | tf_op jit(solution)/shard_map/all_to_all | solution.py:65
  41.7 11.4 %collective-permute-done = bf16[16,8,3200]{2,1,0:T(8,128)(2,1)S(1)} collective-permute-done((bf16[16,8,3200]{2,1,0:T(8,128)(2,1)}, bf16[16,8,3200]{2,1,0:T(8,128)(2,1)S(1)}, u32[]{:S(2)}, u32[]{:S(2)}) %collective-permute-start) | collective-permute-done | bytes 819232 | tf_op jit(solution)/shard_map/ppermute | solution.py:71
  53.2 20.8 %collective-permute-done.1 = bf16[16,8,3200]{2,1,0:T(8,128)(2,1)S(1)} collective-permute-done((bf16[16,8,3200]{2,1,0:T(8,128)(2,1)S(1)}, bf16[16,8,3200]{2,1,0:T(8,128)(2,1)S(1)}, u32[]{:S(2)}, u32[]{:S(2)}) %collective-permute-start.1) | collective-permute-done | bytes 819232 | tf_op jit(solution)/shard_map/ppermute | solution.py:71
  74.1 24.1 %collective-permute-done.2 = bf16[16,8,3200]{2,1,0:T(8,128)(2,1)S(1)} collective-permute-done((bf16[16,8,3200]{2,1,0:T(8,128)(2,1)S(1)}, bf16[16,8,3200]{2,1,0:T(8,128)(2,1)S(1)}, u32[]{:S(2)}, u32[]{:S(2)}) %collective-permute-start.2) | collective-permute-done | bytes 819232 | tf_op jit(solution)/shard_map/ppermute | solution.py:71
  109.0 10.0 %shard_map.458 = (bf16[2,197,2304]{2,1,0:T(8,128)(2,1)}, bf16[2,197,1024]{2,1,0:T(8,128)(2,1)}, f32[128,768]{1,0:T(8,128)}, f32[3,1,3840]{2,1,0:T(1,128)}) custom-call(s32[1]{0:T(128)} %bitcast.core_ref, bf16[64,8,3200]{2,1,0:T(8,128)(2,1)} %bitcast.98, bf16[64,8,3200]{2,1,0:T(8,128)(2,1)} %collective-permute-done.3.other_ref.small_other_ref, ...), custom_call_target="tpu_custom_call" | custom-call | flops 2420736000 | bytes 2000000000 | tf_op jit(solution)/shard_map/pallas_call | solution.py:501
  119.0 13.7 %shard_map.459 = (bf16[2,197,1024]{2,1,0:T(8,128)(2,1)}, f32[2,197,768]{2,1,0:T(8,128)}, bf16[2,197,1024]{2,1,0:T(8,128)(2,1)}, f32[2,197,3]{2,1,0:T(8,128)}, f32[2,197,3]{2,1,0:T(8,128)}) custom-call(s32[1]{0:T(128)} %bitcast.core_ref, bf16[64,8,3200]{2,1,0:T(8,128)(2,1)} %bitcast.100, ...), custom_call_target="tpu_custom_call" | custom-call | flops 1936588800 | bytes 2000000000 | tf_op jit(solution)/shard_map/pallas_call | solution.py:501
  134.8 21.2 %shard_map.460 = (bf16[64,7,8,768]{3,2,1,0:T(8,128)(2,1)}, bf16[64,7,8,768]{3,2,1,0:T(8,128)(2,1)}, f32[1,3072]{1,0:T(1,128)}, f32[1,768]{1,0:T(1,128)}, f32[2,1...) custom-call(s32[1]{0:T(128)} %bitcast.core_ref, bf16[128,3,7,8,768]{4,3,2,1,0:T(8,128)(2,1)} %bitcast.79, ...), custom_call_target="tpu_custom_call" | custom-call | flops 9024307200 | bytes 2000000000 | tf_op jit(solution)/shard_map/pallas_call | solution.py:501
  156.4 21.5 %shard_map.461 = (bf16[64,7,8,768]{3,2,1,0:T(8,128)(2,1)}, bf16[64,7,8,768]{3,2,1,0:T(8,128)(2,1)}, f32[1,3072]{1,0:T(1,128)}, f32[1,768]{1,0:T(1,128)}, f32[2,1...) custom-call(s32[1]{0:T(128)} %bitcast.core_ref, bf16[128,3,7,8,768]{4,3,2,1,0:T(8,128)(2,1)} %bitcast.81, ...), custom_call_target="tpu_custom_call" | custom-call | flops 9024307200 | bytes 2000000000 | tf_op jit(solution)/shard_map/pallas_call | solution.py:501
  182.6 21.9 %shard_map.463 = (bf16[64,7,8,768]{3,2,1,0:T(8,128)(2,1)}, bf16[64,7,8,768]{3,2,1,0:T(8,128)(2,1)}, f32[1,3072]{1,0:T(1,128)}, f32[1,768]{1,0:T(1,128)}, f32[2,1...) custom-call(s32[1]{0:T(128)} %bitcast.core_ref, bf16[128,3,7,8,768]{4,3,2,1,0:T(8,128)(2,1)} %bitcast.83, ...), custom_call_target="tpu_custom_call" | custom-call | flops 9024307200 | bytes 2000000000 | tf_op jit(solution)/shard_map/pallas_call | solution.py:501
  205.6 5.7 %shard_map.464 = (bf16[4,4,7,8,768]{4,3,2,1,0:T(8,128)(2,1)}, bf16[4,4,7,8,768]{4,3,2,1,0:T(8,128)(2,1)}, bf16[64,7,8,768]{3,2,1,0:T(8,128)(2,1)}) custom-call(s32[2]{0:T(128)} %pad_add_fusion.index_ref, bf16[4,4,4,7,8,768]{5,4,3,2,1,0:T(8,128)(2,1)} %bitcast.94, bf16[4,4,4,7,8,768]{5,4,3,2,1,0:T(8,128)(2,1)} %bitcast.15.refs_1_, ...), custom_call_target="tpu_custom_call", output_to_operand_aliasing={{2}: (7, {})} | custom-call | bytes 11000000 | tf_op jit(solution)/shard_map/pallas_call | solution.py:139
  215.2 11.5 %shard_map.465 = (f32[2,197,768]{2,1,0:T(8,128)}, bf16[2,197,768]{2,1,0:T(8,128)(2,1)}, bf16[64,8,768]{2,1,0:T(8,128)(2,1)}, bf16[64,8,768]{2,1,0:T(8,128)(2,1)}, f32[8,768]{1,0:T(8,128)}) custom-call(s32[1]{0:T(128)} %bitcast.core_ref, bf16[64,8,3200]{2,1,0:T(8,128)(2,1)} %bitcast.101, ...), custom_call_target="tpu_custom_call" | custom-call | flops 3227648000 | bytes 2000000000 | tf_op jit(solution)/shard_map/pallas_call | solution.py:501
  226.7 4.6 collective-permute-done.7.refs_2_
  234.2 7.4 %shard_map.466 = (bf16[4,4,7,8,768]{4,3,2,1,0:T(8,128)(2,1)}, bf16[4,4,7,8,768]{4,3,2,1,0:T(8,128)(2,1)}, bf16[4,4,7,8,768]{4,3,2,1,0:T(8,128)(2,1)}) custom-call(s32[3]{0:T(128)} %pad_add_fusion.1.index_ref, bf16[4,4,4,7,8,768]{5,4,3,2,1,0:T(8,128)(2,1)} %bitcast.95, bf16[4,4,4,7,8,768]{5,4,3,2,1,0:T(8,128)(2,1)} %bitcast.15.refs_1_, ...), custom_call_target="tpu_custom_call" | custom-call | bytes 16500000 | tf_op jit(solution)/shard_map/pallas_call | solution.py:139
  244.2 8.9 %shard_map.467.rest_0_.qkv_grad0_ref = bf16[197,2304]{1,0:T(8,128)(2,1)} custom-call(bf16[2,197,2304]{2,1,0:T(8,128)(2,1)} %get-tuple-element.91.qkv_ref, bf16[2,197,768]{2,1,0:T(8,128)(2,1)} %get-tuple-element.116.grad_ref, bf16[4,4,7,8,768]{4,3,2,1,0:T(8,128)(2,1)} %get-tuple-element.120.rest_0_, bf16[4,4,7,8,768]{4,3,2,1,0:T(8,128)(2,1)} %get-tuple-element.121.rest_1_, ...), custom_call_target="tpu_custom_call" | custom-call | flops 1613824000 | bytes 2000000000 | tf_op jit(solution)/shard_map/pallas_call | solution.py:501
  253.1 8.9 %shard_map.468.refs_9_.qkv_grad1_ref = bf16[197,2304]{1,0:T(8,128)(2,1)} custom-call(bf16[2,197,2304]{2,1,0:T(8,128)(2,1)} %get-tuple-element.91.qkv_ref, bf16[2,197,768]{2,1,0:T(8,128)(2,1)} %get-tuple-element.116.grad_ref, bf16[197,2304]{1,0:T(8,128)(2,1)} %shard_map.467.rest_0_.qkv_grad0_ref), custom_call_target="tpu_custom_call" | custom-call | flops 1613824000 | bytes 2000000000 | tf_op jit(solution)/shard_map/pallas_call | solution.py:501
  263.5 8.0 %shard_map.469 = (bf16[4,4,7,8,768]{4,3,2,1,0:T(8,128)(2,1)}, bf16[4,4,7,8,768]{4,3,2,1,0:T(8,128)(2,1)}, bf16[4,4,7,8,768]{4,3,2,1,0:T(8,128)(2,1)}) custom-call(s32[3]{0:T(128)} %pad_add_fusion.2.index_ref, bf16[4,4,4,7,8,768]{5,4,3,2,1,0:T(8,128)(2,1)} %bitcast.96, bf16[4,4,4,7,8,768]{5,4,3,2,1,0:T(8,128)(2,1)} %bitcast.15.refs_1_, ...), custom_call_target="tpu_custom_call" | custom-call | bytes 16500000 | tf_op jit(solution)/shard_map/pallas_call | solution.py:139
  274.6 17.2 %shard_map.471 = (bf16[64,8,2304]{2,1,0:T(8,128)(2,1)}, bf16[64,8,2304]{2,1,0:T(8,128)(2,1)}, bf16[64,8,128]{2,1,0:T(8,128)(2,1)}, bf16[64,8,128]{2,1,0:T(8,128)(2,1)}, f32[2,197,768]{2,1,0:T(8,128)}) custom-call(s32[1]{0:T(128)} %bitcast.core_ref, bf16[64,8,3200]{2,1,0:T(8,128)(2,1)} %bitcast.102, ...), custom_call_target="tpu_custom_call" | custom-call | flops 4034560000 | bytes 2000000000 | tf_op jit(solution)/shard_map/pallas_call | solution.py:501
  297.1 18.0 %collective-permute-done.16.refs_2_ = bf16[4,4,7,8,768]{4,3,2,1,0:T(8,128)(2,1)} collective-permute-done((bf16[4,4,7,8,768]{4,3,2,1,0:T(8,128)(2,1)}, bf16[4,4,7,8,768]{4,3,2,1,0:T(8,128)(2,1)}, u32[]{:S(2)}, u32[]{:S(2)}) %collective-permute-start.16) | collective-permute-done | bytes 1376288 | tf_op jit(solution)/shard_map/ppermute | solution.py:95
  315.1 6.1 %shard_map.472 = (bf16[4,4,7,8,768]{4,3,2,1,0:T(8,128)(2,1)}, bf16[4,4,7,8,768]{4,3,2,1,0:T(8,128)(2,1)}) custom-call(s32[2]{0:T(128)} %pad_add_fusion.3.index_ref, bf16[4,4,4,7,8,768]{5,4,3,2,1,0:T(8,128)(2,1)} %bitcast.92, bf16[4,4,4,7,8,768]{5,4,3,2,1,0:T(8,128)(2,1)} %bitcast.19.refs_4_.refs_1_, ...), custom_call_target="tpu_custom_call" | custom-call | bytes 11000000 | tf_op jit(solution)/shard_map/pallas_call | solution.py:139
  323.1 5.1 %shard_map.473 = bf16[64,8,3200]{2,1,0:T(8,128)(2,1)} custom-call(bf16[64,8,2304]{2,1,0:T(8,128)(2,1)} %get-tuple-element.133.own_qkv, bf16[64,8,2304]{2,1,0:T(8,128)(2,1)} %copy-done.1, bf16[64,8,768]{2,1,0:T(8,128)(2,1)} %get-tuple-element.135.own_out, bf16[64,8,768]{2,1,0:T(8,128)(2,1)} %copy-done.16, ...), custom_call_target="tpu_custom_call" | custom-call | bytes 2000000000 | tf_op jit(solution)/shard_map/pallas_call | solution.py:501
  332.9 12.5 %collective-permute-done.18.refs_1_ = bf16[4,4,8,3200]{3,2,1,0:T(8,128)(2,1)S(1)} collective-permute-done((bf16[4,4,8,3200]{3,2,1,0:T(8,128)(2,1)}, bf16[4,4,8,3200]{3,2,1,0:T(8,128)(2,1)S(1)}, u32[]{:S(2)}, u32[]{:S(2)}) %collective-permute-start.18) | collective-permute-done | bytes 819232 | tf_op jit(solution)/shard_map/ppermute | solution.py:95
  351.3 7.1 %collective-permute-done.21.refs_1_ = bf16[4,7,8,768]{3,2,1,0:T(8,128)(2,1)S(1)} collective-permute-done((bf16[4,7,8,768]{3,2,1,0:T(8,128)(2,1)S(1)}, bf16[4,7,8,768]{3,2,1,0:T(8,128)(2,1)S(1)}, u32[]{:S(2)}, u32[]{:S(2)}) %collective-permute-start.21) | collective-permute-done | bytes 344096 | tf_op jit(solution)/shard_map/ppermute | solution.py:95
  360.2 5.2 %shard_map.478 = (bf16[4,7,8,768]{3,2,1,0:T(8,128)(2,1)}, bf16[4,7,8,768]{3,2,1,0:T(8,128)(2,1)}, bf16[4,4,7,8,768]{4,3,2,1,0:T(8,128)(2,1)}) custom-call(s32[3]{0:T(128)} %pad_add_fusion.6.index_ref, bf16[4,4,7,8,768]{4,3,2,1,0:T(8,128)(2,1)} %get-tuple-element.131.refs_0_, bf16[4,7,8,768]{3,2,1,0:T(8,128)(2,1)} %copy-done.29, ...), custom_call_target="tpu_custom_call" | custom-call | bytes 16500000 | tf_op jit(solution)/shard_map/pallas_call | solution.py:139
  374.9 4.3 shard_map.479
  383.1 4.8 %collective-permute-done.25.refs_1_ = bf16[4,7,8,768]{3,2,1,0:T(8,128)(2,1)S(1)} collective-permute-done((bf16[4,7,8,768]{3,2,1,0:T(8,128)(2,1)}, bf16[4,7,8,768]{3,2,1,0:T(8,128)(2,1)S(1)}, u32[]{:S(2)}, u32[]{:S(2)}) %collective-permute-start.25) | collective-permute-done | bytes 344096 | tf_op jit(solution)/shard_map/ppermute | solution.py:95
  392.3 4.3 shard_map.480
  407.1 4.1 all-to-all-start.1
  419.4 4.9 %collective-permute-done.28.refs_1_ = bf16[4,7,8,768]{3,2,1,0:T(8,128)(2,1)S(1)} collective-permute-done((bf16[4,7,8,768]{3,2,1,0:T(8,128)(2,1)}, bf16[4,7,8,768]{3,2,1,0:T(8,128)(2,1)S(1)}, u32[]{:S(2)}, u32[]{:S(2)}) %collective-permute-start.28) | collective-permute-done | bytes 344096 | tf_op jit(solution)/shard_map/ppermute | solution.py:95
  425.9 4.1 shard_map.481
  431.6 7.2 %collective-permute-done.30.refs_1_ = bf16[4,7,8,768]{3,2,1,0:T(8,128)(2,1)S(1)} collective-permute-done((bf16[4,7,8,768]{3,2,1,0:T(8,128)(2,1)}, bf16[4,7,8,768]{3,2,1,0:T(8,128)(2,1)S(1)}, u32[]{:S(2)}, u32[]{:S(2)}) %collective-permute-start.30) | collective-permute-done | bytes 344096 | tf_op jit(solution)/shard_map/ppermute | solution.py:95
  444.8 4.4 all-to-all-start.3
  (250 shorter events, 120.3 us)
Async XLA Ops:
  7.2 127.6 %all-gather.3.cloned.1.call-start = ((), (), s32[]{:S(2)}) async-start(), calls=%async_computation.4 | async-start | bytes 33288192 | tf_op jit(solution)/shard_map/all_gather | solution.py:559
  14.8 23.5 %all-to-all-start = ((bf16[16,8,3200]{2,1,0:T(8,128)(2,1)}), bf16[16,8,3200]{2,1,0:T(8,128)(2,1)}, u32[]{:S(2)}, u32[]{:S(2)}) async-start(bf16[16,8,3200]{2,1,0:T(8,128)(2,1)} %broadcast_in_dim.38), calls=%async_computation | async-start | bytes 1638400 | tf_op jit(solution)/shard_map/all_to_all | solution.py:65
  38.3 14.8 %collective-permute-start = (bf16[16,8,3200]{2,1,0:T(8,128)(2,1)}, bf16[16,8,3200]{2,1,0:T(8,128)(2,1)S(1)}, u32[]{:S(2)}, u32[]{:S(2)}) collective-permute-start(bf16[16,8,3200]{2,1,0:T(8,128)(2,1)} %all-to-all-done), channel_id=1, source_target_pairs={{0,32},{32,64},{64,96},{96,0},{1,97},{33,1},{65,33},{97,65},{2,34}... | collective-permute-start | bytes 2457608 | tf_op jit(solution)/shard_map/ppermute | solution.py:71
  53.1 20.9 %collective-permute-start.1 = (bf16[16,8,3200]{2,1,0:T(8,128)(2,1)S(1)}, bf16[16,8,3200]{2,1,0:T(8,128)(2,1)S(1)}, u32[]{:S(2)}, u32[]{:S(2)}) collective-permute-start(bf16[16,8,3200]{2,1,0:T(8,128)(2,1)S(1)} %collective-permute-done), channel_id=1, source_target_pairs={{0,32},{32,64},{64,96},{96,0},{1,97},{33,1},{65,33},{97,65},{2,34}... | collective-permute-start | bytes 2457608 | tf_op jit(solution)/shard_map/ppermute | solution.py:71
  74.0 24.2 %collective-permute-start.2 = (bf16[16,8,3200]{2,1,0:T(8,128)(2,1)S(1)}, bf16[16,8,3200]{2,1,0:T(8,128)(2,1)S(1)}, u32[]{:S(2)}, u32[]{:S(2)}) collective-permute-start(bf16[16,8,3200]{2,1,0:T(8,128)(2,1)S(1)} %collective-permute-done.1), channel_id=1, source_target_pairs={{0,32},{32,64},{64,96},{96,0},{1,97},{33,1},{65,33},{97,65},{2,34}... | collective-permute-start | bytes 2457608 | tf_op jit(solution)/shard_map/ppermute | solution.py:71
  98.3 10.6 %collective-permute-start.3 = (bf16[64,8,3200]{2,1,0:T(8,128)(2,1)S(1)}, bf16[64,8,3200]{2,1,0:T(8,128)(2,1)}, u32[]{:S(2)}, u32[]{:S(2)}) collective-permute-start(bf16[64,8,3200]{2,1,0:T(8,128)(2,1)S(1)} %bitcast.97), channel_id=1, source_target_pairs={{0,1},{1,0},{2,3},{3,2},{4,5},{5,4},{6,7},{7,6},{8,9},{9,8},{10,11... | collective-permute-start | bytes 9830408 | tf_op jit(solution)/shard_map/ppermute | solution.py:51
  156.0 21.9 %collective-permute-start.4 = (bf16[64,7,8,768]{3,2,1,0:T(8,128)(2,1)}, bf16[64,7,8,768]{3,2,1,0:T(8,128)(2,1)}, u32[]{:S(2)}, u32[]{:S(2)}) collective-permute-start(bf16[64,7,8,768]{3,2,1,0:T(8,128)(2,1)} %get-tuple-element.101), channel_id=1, source_target_pairs={{0,1},{1,0},{2,3},{3,2},{4,5},{5,4},{6,7},{7,6},{8,9},{9,8},{10,11... | collective-permute-start | bytes 16515080 | tf_op jit(solution)/shard_map/ppermute | solution.py:51
  181.8 22.8 %collective-permute-start.6 = (bf16[64,7,8,768]{3,2,1,0:T(8,128)(2,1)}, bf16[64,7,8,768]{3,2,1,0:T(8,128)(2,1)}, u32[]{:S(2)}, u32[]{:S(2)}) collective-permute-start(bf16[64,7,8,768]{3,2,1,0:T(8,128)(2,1)} %get-tuple-element.112), channel_id=1, source_target_pairs={{0,1},{1,0},{2,3},{3,2},{4,5},{5,4},{6,7},{7,6},{8,9},{9,8},{10,11... | collective-permute-start | bytes 16515080 | tf_op jit(solution)/shard_map/ppermute | solution.py:51
  182.0 22.5 %collective-permute-start.5 = (bf16[4,4,7,8,768]{4,3,2,1,0:T(8,128)(2,1)}, bf16[4,4,7,8,768]{4,3,2,1,0:T(8,128)(2,1)S(1)}, u32[]{:S(2)}, u32[]{:S(2)}) collective-permute-start(bf16[4,4,7,8,768]{4,3,2,1,0:T(8,128)(2,1)} %get-tuple-element.104.rest_1_), channel_id=1, source_target_pairs={{0,32},{32,64},{64,96},{96,0},{1,97},{33,1},{65,33},{97,65},{2,34}... | collective-permute-start | bytes 4128776 | tf_op jit(solution)/shard_map/ppermute | solution.py:95
  211.3 21.7 %collective-permute-start.9 = (bf16[64,7,8,768]{3,2,1,0:T(8,128)(2,1)}, bf16[64,7,8,768]{3,2,1,0:T(8,128)(2,1)}, u32[]{:S(2)}, u32[]{:S(2)}) collective-permute-start(bf16[64,7,8,768]{3,2,1,0:T(8,128)(2,1)} %get-tuple-element.118), channel_id=1, source_target_pairs={{0,1},{1,0},{2,3},{3,2},{4,5},{5,4},{6,7},{7,6},{8,9},{9,8},{10,11... | collective-permute-start | bytes 16515080 | tf_op jit(solution)/shard_map/ppermute | solution.py:51
  211.6 19.7 %collective-permute-start.7 = (bf16[4,4,7,8,768]{4,3,2,1,0:T(8,128)(2,1)}, bf16[4,4,7,8,768]{4,3,2,1,0:T(8,128)(2,1)S(1)}, u32[]{:S(2)}, u32[]{:S(2)}) collective-permute-start(bf16[4,4,7,8,768]{4,3,2,1,0:T(8,128)(2,1)} %get-tuple-element.114.rest_0_), channel_id=1, source_target_pairs={{0,32},{32,64},{64,96},{96,0},{1,97},{33,1},{65,33},{97,65},{2,34}... | collective-permute-start | bytes 4128776 | tf_op jit(solution)/shard_map/ppermute | solution.py:95
  213.3 19.7 %collective-permute-start.8 = (bf16[4,4,7,8,768]{4,3,2,1,0:T(8,128)(2,1)}, bf16[4,4,7,8,768]{4,3,2,1,0:T(8,128)(2,1)S(1)}, u32[]{:S(2)}, u32[]{:S(2)}) collective-permute-start(bf16[4,4,7,8,768]{4,3,2,1,0:T(8,128)(2,1)} %get-tuple-element.115.rest_1_), channel_id=1, source_target_pairs={{0,8},{8,16},{16,24},{24,0},{1,25},{9,1},{17,9},{25,17},{2,10},{10... | collective-permute-start | bytes 4128776 | tf_op jit(solution)/shard_map/ppermute | solution.py:95
  241.6 20.4 %collective-permute-start.10 = (bf16[4,4,7,8,768]{4,3,2,1,0:T(8,128)(2,1)}, bf16[4,4,7,8,768]{4,3,2,1,0:T(8,128)(2,1)S(1)}, u32[]{:S(2)}, u32[]{:S(2)}) collective-permute-start(bf16[4,4,7,8,768]{4,3,2,1,0:T(8,128)(2,1)} %get-tuple-element.120.rest_0_), channel_id=1, source_target_pairs={{0,32},{32,64},{64,96},{96,0},{1,97},{33,1},{65,33},{97,65},{2,34}... | collective-permute-start | bytes 4128776 | tf_op jit(solution)/shard_map/ppermute | solution.py:95
  241.6 20.4 %collective-permute-start.11 = (bf16[4,4,7,8,768]{4,3,2,1,0:T(8,128)(2,1)}, bf16[4,4,7,8,768]{4,3,2,1,0:T(8,128)(2,1)S(1)}, u32[]{:S(2)}, u32[]{:S(2)}) collective-permute-start(bf16[4,4,7,8,768]{4,3,2,1,0:T(8,128)(2,1)} %get-tuple-element.121.rest_1_), channel_id=1, source_target_pairs={{0,8},{8,16},{16,24},{24,0},{1,25},{9,1},{17,9},{25,17},{2,10},{10... | collective-permute-start | bytes 4128776 | tf_op jit(solution)/shard_map/ppermute | solution.py:95
  242.2 19.9 %collective-permute-start.12 = (bf16[4,4,7,8,768]{4,3,2,1,0:T(8,128)(2,1)}, bf16[4,4,7,8,768]{4,3,2,1,0:T(8,128)(2,1)}, u32[]{:S(2)}, u32[]{:S(2)}) collective-permute-start(bf16[4,4,7,8,768]{4,3,2,1,0:T(8,128)(2,1)} %get-tuple-element.122.rest_2_), channel_id=1, source_target_pairs={{0,2},{2,4},{4,6},{6,0},{1,7},{3,1},{5,3},{7,5},{8,10},{10,12},{12... | collective-permute-start | bytes 4128776 | tf_op jit(solution)/shard_map/ppermute | solution.py:95
  291.8 29.5 %collective-permute-start.13 = (bf16[64,8,2304]{2,1,0:T(8,128)(2,1)}, bf16[64,8,2304]{2,1,0:T(8,128)(2,1)S(1)}, u32[]{:S(2)}, u32[]{:S(2)}) collective-permute-start(bf16[64,8,2304]{2,1,0:T(8,128)(2,1)} %get-tuple-element.134), channel_id=1, source_target_pairs={{0,1},{1,0},{2,3},{3,2},{4,5},{5,4},{6,7},{7,6},{8,9},{9,8},{10,11... | collective-permute-start | bytes 7077896 | tf_op jit(solution)/shard_map/ppermute | solution.py:51
  295.3 19.8 %collective-permute-start.16 = (bf16[4,4,7,8,768]{4,3,2,1,0:T(8,128)(2,1)}, bf16[4,4,7,8,768]{4,3,2,1,0:T(8,128)(2,1)}, u32[]{:S(2)}, u32[]{:S(2)}) collective-permute-start(bf16[4,4,7,8,768]{4,3,2,1,0:T(8,128)(2,1)} %get-tuple-element.139), channel_id=1, source_target_pairs={{0,8},{8,16},{16,24},{24,0},{1,25},{9,1},{17,9},{25,17},{2,10},{10... | collective-permute-start | bytes 4128776 | tf_op jit(solution)/shard_map/ppermute | solution.py:95
  295.3 19.8 %collective-permute-start.17 = (bf16[4,4,7,8,768]{4,3,2,1,0:T(8,128)(2,1)}, bf16[4,4,7,8,768]{4,3,2,1,0:T(8,128)(2,1)}, u32[]{:S(2)}, u32[]{:S(2)}) collective-permute-start(bf16[4,4,7,8,768]{4,3,2,1,0:T(8,128)(2,1)} %get-tuple-element.140), channel_id=1, source_target_pairs={{0,2},{2,4},{4,6},{6,0},{1,7},{3,1},{5,3},{7,5},{8,10},{10,12},{12... | collective-permute-start | bytes 4128776 | tf_op jit(solution)/shard_map/ppermute | solution.py:95
  295.3 26.0 %collective-permute-start.14 = (bf16[64,8,768]{2,1,0:T(8,128)(2,1)}, bf16[64,8,768]{2,1,0:T(8,128)(2,1)S(1)}, u32[]{:S(2)}, u32[]{:S(2)}) collective-permute-start(bf16[64,8,768]{2,1,0:T(8,128)(2,1)} %get-tuple-element.136), channel_id=1, source_target_pairs={{0,1},{1,0},{2,3},{3,2},{4,5},{5,4},{6,7},{7,6},{8,9},{9,8},{10,11... | collective-permute-start | bytes 2359304 | tf_op jit(solution)/shard_map/ppermute | solution.py:51
  296.5 24.8 %collective-permute-start.15 = (bf16[64,8,128]{2,1,0:T(8,128)(2,1)}, bf16[64,8,128]{2,1,0:T(8,128)(2,1)S(1)}, u32[]{:S(2)}, u32[]{:S(2)}) collective-permute-start(bf16[64,8,128]{2,1,0:T(8,128)(2,1)} %get-tuple-element.138), channel_id=1, source_target_pairs={{0,1},{1,0},{2,3},{3,2},{4,5},{5,4},{6,7},{7,6},{8,9},{9,8},{10,11... | collective-permute-start | bytes 393224 | tf_op jit(solution)/shard_map/ppermute | solution.py:51
  331.6 13.8 %collective-permute-start.18 = (bf16[4,4,8,3200]{3,2,1,0:T(8,128)(2,1)}, bf16[4,4,8,3200]{3,2,1,0:T(8,128)(2,1)S(1)}, u32[]{:S(2)}, u32[]{:S(2)}) collective-permute-start(bf16[4,4,8,3200]{3,2,1,0:T(8,128)(2,1)} %shard_map.474.refs_6_), channel_id=1, source_target_pairs={{0,32},{32,64},{64,96},{96,0},{1,97},{33,1},{65,33},{97,65},{2,34}... | collective-permute-start | bytes 2457608 | tf_op jit(solution)/shard_map/ppermute | solution.py:95
  332.9 25.5 %collective-permute-start.22 = (bf16[4,4,7,8,768]{4,3,2,1,0:T(8,128)(2,1)S(1)}, bf16[4,4,7,8,768]{4,3,2,1,0:T(8,128)(2,1)S(1)}, u32[]{:S(2)}, u32[]{:S(2)}) collective-permute-start(bf16[4,4,7,8,768]{4,3,2,1,0:T(8,128)(2,1)S(1)} %copy-done.5), channel_id=1, source_target_pairs={{0,2},{2,4},{4,6},{6,0},{1,7},{3,1},{5,3},{7,5},{8,10},{10,12},{12... | collective-permute-start | bytes 4128776 | tf_op jit(solution)/shard_map/ppermute | solution.py:95
  349.8 15.6 %collective-permute-start.19 = (bf16[4,4,8,3200]{3,2,1,0:T(8,128)(2,1)}, bf16[4,4,8,3200]{3,2,1,0:T(8,128)(2,1)}, u32[]{:S(2)}, u32[]{:S(2)}) collective-permute-start(bf16[4,4,8,3200]{3,2,1,0:T(8,128)(2,1)} %shard_map.475.refs_5_), channel_id=1, source_target_pairs={{0,32},{32,64},{64,96},{96,0},{1,97},{33,1},{65,33},{97,65},{2,34}... | collective-permute-start | bytes 2457608 | tf_op jit(solution)/shard_map/ppermute | solution.py:95
  365.3 8.7 %collective-permute-start.24 = (bf16[4,7,8,768]{3,2,1,0:T(8,128)(2,1)}, bf16[4,7,8,768]{3,2,1,0:T(8,128)(2,1)S(1)}, u32[]{:S(2)}, u32[]{:S(2)}) collective-permute-start(bf16[4,7,8,768]{3,2,1,0:T(8,128)(2,1)} %get-tuple-element.144), channel_id=1, source_target_pairs={{0,2},{2,4},{4,6},{6,0},{1,7},{3,1},{5,3},{7,5},{8,10},{10,12},{12... | collective-permute-start | bytes 1032200 | tf_op jit(solution)/shard_map/ppermute | solution.py:95
  369.0 31.1 %collective-permute-start.20 = (bf16[4,4,8,3200]{3,2,1,0:T(8,128)(2,1)}, bf16[4,4,8,3200]{3,2,1,0:T(8,128)(2,1)S(1)}, u32[]{:S(2)}, u32[]{:S(2)}) collective-permute-start(bf16[4,4,8,3200]{3,2,1,0:T(8,128)(2,1)} %shard_map.476.refs_6_), channel_id=1, source_target_pairs={{0,32},{32,64},{64,96},{96,0},{1,97},{33,1},{65,33},{97,65},{2,34}... | collective-permute-start | bytes 2457608 | tf_op jit(solution)/shard_map/ppermute | solution.py:95
  379.1 8.7 %collective-permute-start.25 = (bf16[4,7,8,768]{3,2,1,0:T(8,128)(2,1)}, bf16[4,7,8,768]{3,2,1,0:T(8,128)(2,1)S(1)}, u32[]{:S(2)}, u32[]{:S(2)}) collective-permute-start(bf16[4,7,8,768]{3,2,1,0:T(8,128)(2,1)} %get-tuple-element.146), channel_id=1, source_target_pairs={{0,8},{8,16},{16,24},{24,0},{1,25},{9,1},{17,9},{25,17},{2,10},{10... | collective-permute-start | bytes 1032200 | tf_op jit(solution)/shard_map/ppermute | solution.py:95
  380.1 11.4 %collective-permute-start.27 = (bf16[4,7,8,768]{3,2,1,0:T(8,128)(2,1)}, bf16[4,7,8,768]{3,2,1,0:T(8,128)(2,1)S(1)}, u32[]{:S(2)}, u32[]{:S(2)}) collective-permute-start(bf16[4,7,8,768]{3,2,1,0:T(8,128)(2,1)} %get-tuple-element.148), channel_id=1, source_target_pairs={{0,8},{8,16},{16,24},{24,0},{1,25},{9,1},{17,9},{25,17},{2,10},{10... | collective-permute-start | bytes 1032200 | tf_op jit(solution)/shard_map/ppermute | solution.py:95
  396.6 10.5 %all-to-all-start.2 = ((bf16[4,7,8,768]{3,2,1,0:T(8,128)(2,1)}), bf16[4,7,8,768]{3,2,1,0:T(8,128)(2,1)S(1)}, u32[]{:S(2)}, u32[]{:S(2)}) async-start(bf16[4,7,8,768]{3,2,1,0:T(8,128)(2,1)} %get-tuple-element.149), calls=%async_computation.2 | async-start | bytes 688128 | tf_op jit(solution)/shard_map/all_to_all | solution.py:109
  407.1 24.3 %all-to-all-start.1 = ((bf16[16,8,3200]{2,1,0:T(8,128)(2,1)}), bf16[16,8,3200]{2,1,0:T(8,128)(2,1)S(1)}, u32[]{:S(2)}, u32[]{:S(2)}) async-start(bf16[16,8,3200]{2,1,0:T(8,128)(2,1)} %bitcast.107), calls=%async_computation.1 | async-start | bytes 1638400 | tf_op jit(solution)/shard_map/all_to_all | solution.py:109
  411.3 13.0 %collective-permute-start.28 = (bf16[4,7,8,768]{3,2,1,0:T(8,128)(2,1)}, bf16[4,7,8,768]{3,2,1,0:T(8,128)(2,1)S(1)}, u32[]{:S(2)}, u32[]{:S(2)}) collective-permute-start(bf16[4,7,8,768]{3,2,1,0:T(8,128)(2,1)} %get-tuple-element.150), channel_id=1, source_target_pairs={{0,2},{2,4},{4,6},{6,0},{1,7},{3,1},{5,3},{7,5},{8,10},{10,12},{12... | collective-permute-start | bytes 1032200 | tf_op jit(solution)/shard_map/ppermute | solution.py:95
  413.2 12.0 %collective-permute-start.29 = (bf16[4,7,8,768]{3,2,1,0:T(8,128)(2,1)}, bf16[4,7,8,768]{3,2,1,0:T(8,128)(2,1)S(1)}, u32[]{:S(2)}, u32[]{:S(2)}) collective-permute-start(bf16[4,7,8,768]{3,2,1,0:T(8,128)(2,1)} %get-tuple-element.151), channel_id=1, source_target_pairs={{0,8},{8,16},{16,24},{24,0},{1,25},{9,1},{17,9},{25,17},{2,10},{10... | collective-permute-start | bytes 1032200 | tf_op jit(solution)/shard_map/ppermute | solution.py:95
  444.8 13.4 %all-to-all-start.3 = ((bf16[4,14,8,768]{3,2,1,0:T(8,128)(2,1)}), bf16[4,14,8,768]{3,2,1,0:T(8,128)(2,1)S(1)}, u32[]{:S(2)}, u32[]{:S(2)}) async-start(bf16[4,14,8,768]{3,2,1,0:T(8,128)(2,1)} %pad_maximum_fusion), calls=%async_computation.3 | async-start | bytes 1376256 | tf_op jit(solution)/shard_map/all_to_all | solution.py:109
  (57 other events, 387.5 us)
Sparse Core Ops, SparseCore 0:
  11.6 123.1 all-gather.2
where the time goes:
time: 473 us; the launch traced here: 468 us
  Pallas kernels  209 us (44%)
  waiting for transfers between devices  148 us (31%)
  starting transfers between devices  42.6 us (9%)
  local copies, waits for them, and re-layouts  36.1 us (8%)
  other arithmetic  17 us (4%)
  between operations  15 us (3%)
    pallas_call x10, Pallas kernels, call(): pl.pallas_call(kernel, grid=grid, in_specs=in_specs, out_specs=[spec(shap...  140 us
    ppermute x21, waiting for transfers between devices, pass_on(): return lax.ppermute(self.piece, (self.axes[0], CORE), ring_pairs())  69.6 us
    pallas_call x15, Pallas kernels, next_round(): pl.pallas_call(functools.partial(round_kernel, sizes, len(carry)), grid_s...  69.3 us
    ppermute x3, waiting for transfers between devices, chips_gather(): moving = lax.ppermute(moving, (CHIPS[0], CORE), ring_pairs())  56.3 us
    unnamed x130, local copies, waits for them, and re-layouts  27.4 us
    all_to_all x1, waiting for transfers between devices, chips_gather(): lax.all_to_all(jnp.broadcast_to(x, (16, *x.shape)), CHIPS[1:], 0, 0, tile...  16.3 us
    ppermute x21, starting transfers between devices, pass_on(): return lax.ppermute(self.piece, (self.axes[0], CORE), ring_pairs())  15.6 us
    all_to_all x3, starting transfers between devices, totals(): blocks = lax.all_to_all(blocks, tuple(rings[0].names), 0, 0, tiled=True)  12 us
  transfers between devices with their start and end apart: 36, of which 20 were waited for; matrix products, arithmetic and copies ran while one was open for 7% of the time, Pallas kernels for 28%

commit v1 on v0

--- a/solution.py
+++ b/solution.py
@@ -723,7 +723,7 @@
         flops=2 * 394 * 1024 * 5000,
     )
 
-    follow = next_round(rings[1:], (own_small,))
+    follow = next_round(rings, (own_small,))
     def chips_part(n):
         return (16, 8, n), lambda i: (i, 0, 0)
 
@@ -737,14 +737,15 @@
         [((64, 8, 3200), bf, *chips_part(3200))],
         after=follow,
     )[0]
-    attn_ring = Ring((pair,), 0)
-    for _ in range(3):
-        next_round(rings, next_round([attn_ring]))
-    next_round([attn_ring])
-    attn_sum = attn_ring.total()
-    next_round(rings[1:], (attn_ring.piece,))
-    next_round(rings[2:], (attn_sum,))
-    expert_sums = [rings[0].total(), *totals(rings[1:])]
+    rings.append(Ring((pair,), 0))
+    next_round(rings)
+    next_round(rings)
+    expert_sums = [rings[0].total()]
+    next_round(rings[1:])
+    next_round(rings[1:], expert_sums[:1])
+    attn_sum = rings[3].total()
+    next_round(rings[2:3])
+    expert_sums += totals(rings[1:3])
     ebias_sum = attn_sum[6, 3072:3168].reshape(3, 32)[:, :30]
     attn_sum = attn_sum[:6]
     small_sum = attn_sum[:, 3072:]

time: 473 us -> 448 us (0.947)
  Pallas kernels: 209 us -> 197 us
  waiting for transfers between devices: 148 us -> 140 us
    pallas_call x15 -> x11, Pallas kernels: 69.3 us -> 57.1 us  [next_round(): pl.pallas_call(functools.partial(round_kernel, sizes, len(carry)), grid_s...]
    ppermute x21, waiting for transfers between devices: 69.6 us -> 58.5 us  [pass_on(): return lax.ppermute(self.piece, (self.axes[0], CORE), ring_pairs())]
    unnamed x130 -> x122, local copies, waits for them, and re-layouts: 27.4 us -> 24.9 us
  transfers between devices with their start and end apart: 36 -> 36, of which waited for: 20 -> 21; matrix products, arithmetic and copies ran while one was open for 7% -> 8% of each run, Pallas kernels for 28% -> 30%
where the time goes in v1:
time: 448 us; the launch traced here: 443 us
  Pallas kernels  197 us (44%)
  waiting for transfers between devices  140 us (31%)
  starting transfers between devices  39.6 us (9%)
  local copies, waits for them, and re-layouts  33.6 us (8%)
  other arithmetic  17.6 us (4%)
  between operations  14.9 us (3%)
    pallas_call x10, Pallas kernels, call(): pl.pallas_call(kernel, grid=grid, in_specs=in_specs, out_specs=[spec(shap...  140 us
    ppermute x21, waiting for transfers between devices, pass_on(): return lax.ppermute(self.piece, (self.axes[0], CORE), ring_pairs())  58.5 us
    pallas_call x11, Pallas kernels, next_round(): pl.pallas_call(functools.partial(round_kernel, sizes, len(carry)), grid_s...  57.1 us
    ppermute x3, waiting for transfers between devices, chips_gather(): moving = lax.ppermute(moving, (CHIPS[0], CORE), ring_pairs())  56.3 us
    unnamed x122, local copies, waits for them, and re-layouts  24.9 us
    all_to_all x1, waiting for transfers between devices, chips_gather(): lax.all_to_all(jnp.broadcast_to(x, (16, *x.shape)), CHIPS[1:], 0, 0, tile...  16.3 us
    ppermute x21, starting transfers between devices, pass_on(): return lax.ppermute(self.piece, (self.axes[0], CORE), ring_pairs())  15.9 us
    all_to_all x3, starting transfers between devices, totals(): blocks = lax.all_to_all(blocks, tuple(rings[0].names), 0, 0, tiled=True)  11.3 us
  transfers between devices with their start and end apart: 36, of which 21 were waited for; matrix products, arithmetic and copies ran while one was open for 8% of the time, Pallas kernels for 30%

profile of v1, /device:TPU:0, one launch (start us, length us, event | category | flops | bytes accessed | tf_op | source)
XLA Modules:
  0.0 443.3 jit_solution(17799665526149989302)
XLA Ops:
  14.8 7.2 %all-to-all-start = ((bf16[16,8,3200]{2,1,0:T(8,128)(2,1)}), bf16[16,8,3200]{2,1,0:T(8,128)(2,1)}, u32[]{:S(2)}, u32[]{:S(2)}) async-start(bf16[16,8,3200]{2,1,0:T(8,128)(2,1)} %broadcast_in_dim.38), calls=%async_computation | async-start | bytes 1638400 | tf_op jit(solution)/shard_map/all_to_all | solution.py:65
  22.0 16.3 %all-to-all-done = bf16[16,8,3200]{2,1,0:T(8,128)(2,1)} async-done(((bf16[16,8,3200]{2,1,0:T(8,128)(2,1)}), bf16[16,8,3200]{2,1,0:T(8,128)(2,1)}, u32[]{:S(2)}, u32[]{:S(2)}) %all-to-all-start) | async-done | bytes 819232 | tf_op jit(solution)/shard_map/all_to_all | solution.py:65
  41.7 11.4 %collective-permute-done = bf16[16,8,3200]{2,1,0:T(8,128)(2,1)S(1)} collective-permute-done((bf16[16,8,3200]{2,1,0:T(8,128)(2,1)}, bf16[16,8,3200]{2,1,0:T(8,128)(2,1)S(1)}, u32[]{:S(2)}, u32[]{:S(2)}) %collective-permute-start) | collective-permute-done | bytes 819232 | tf_op jit(solution)/shard_map/ppermute | solution.py:71
  53.2 20.8 %collective-permute-done.1 = bf16[16,8,3200]{2,1,0:T(8,128)(2,1)S(1)} collective-permute-done((bf16[16,8,3200]{2,1,0:T(8,128)(2,1)S(1)}, bf16[16,8,3200]{2,1,0:T(8,128)(2,1)S(1)}, u32[]{:S(2)}, u32[]{:S(2)}) %collective-permute-start.1) | collective-permute-done | bytes 819232 | tf_op jit(solution)/shard_map/ppermute | solution.py:71
  74.1 24.1 %collective-permute-done.2 = bf16[16,8,3200]{2,1,0:T(8,128)(2,1)S(1)} collective-permute-done((bf16[16,8,3200]{2,1,0:T(8,128)(2,1)S(1)}, bf16[16,8,3200]{2,1,0:T(8,128)(2,1)S(1)}, u32[]{:S(2)}, u32[]{:S(2)}) %collective-permute-start.2) | collective-permute-done | bytes 819232 | tf_op jit(solution)/shard_map/ppermute | solution.py:71
  109.0 10.0 %shard_map.458 = (bf16[2,197,2304]{2,1,0:T(8,128)(2,1)}, bf16[2,197,1024]{2,1,0:T(8,128)(2,1)}, f32[128,768]{1,0:T(8,128)}, f32[3,1,3840]{2,1,0:T(1,128)}) custom-call(s32[1]{0:T(128)} %bitcast.core_ref, bf16[64,8,3200]{2,1,0:T(8,128)(2,1)} %bitcast.98, bf16[64,8,3200]{2,1,0:T(8,128)(2,1)} %collective-permute-done.3.other_ref.small_other_ref, ...), custom_call_target="tpu_custom_call" | custom-call | flops 2420736000 | bytes 2000000000 | tf_op jit(solution)/shard_map/pallas_call | solution.py:501
  119.0 13.7 %shard_map.459 = (bf16[2,197,1024]{2,1,0:T(8,128)(2,1)}, f32[2,197,768]{2,1,0:T(8,128)}, bf16[2,197,1024]{2,1,0:T(8,128)(2,1)}, f32[2,197,3]{2,1,0:T(8,128)}, f32[2,197,3]{2,1,0:T(8,128)}) custom-call(s32[1]{0:T(128)} %bitcast.core_ref, bf16[64,8,3200]{2,1,0:T(8,128)(2,1)} %bitcast.100, ...), custom_call_target="tpu_custom_call" | custom-call | flops 1936588800 | bytes 2000000000 | tf_op jit(solution)/shard_map/pallas_call | solution.py:501
  134.8 21.2 %shard_map.460 = (bf16[64,7,8,768]{3,2,1,0:T(8,128)(2,1)}, bf16[64,7,8,768]{3,2,1,0:T(8,128)(2,1)}, f32[1,3072]{1,0:T(1,128)}, f32[1,768]{1,0:T(1,128)}, f32[2,1...) custom-call(s32[1]{0:T(128)} %bitcast.core_ref, bf16[128,3,7,8,768]{4,3,2,1,0:T(8,128)(2,1)} %bitcast.79, ...), custom_call_target="tpu_custom_call" | custom-call | flops 9024307200 | bytes 2000000000 | tf_op jit(solution)/shard_map/pallas_call | solution.py:501
  156.4 21.5 %shard_map.461 = (bf16[64,7,8,768]{3,2,1,0:T(8,128)(2,1)}, bf16[64,7,8,768]{3,2,1,0:T(8,128)(2,1)}, f32[1,3072]{1,0:T(1,128)}, f32[1,768]{1,0:T(1,128)}, f32[2,1...) custom-call(s32[1]{0:T(128)} %bitcast.core_ref, bf16[128,3,7,8,768]{4,3,2,1,0:T(8,128)(2,1)} %bitcast.81, ...), custom_call_target="tpu_custom_call" | custom-call | flops 9024307200 | bytes 2000000000 | tf_op jit(solution)/shard_map/pallas_call | solution.py:501
  182.6 21.9 %shard_map.463 = (bf16[64,7,8,768]{3,2,1,0:T(8,128)(2,1)}, bf16[64,7,8,768]{3,2,1,0:T(8,128)(2,1)}, f32[1,3072]{1,0:T(1,128)}, f32[1,768]{1,0:T(1,128)}, f32[2,1...) custom-call(s32[1]{0:T(128)} %bitcast.core_ref, bf16[128,3,7,8,768]{4,3,2,1,0:T(8,128)(2,1)} %bitcast.83, ...), custom_call_target="tpu_custom_call" | custom-call | flops 9024307200 | bytes 2000000000 | tf_op jit(solution)/shard_map/pallas_call | solution.py:501
  205.6 5.7 %shard_map.464 = (bf16[4,4,7,8,768]{4,3,2,1,0:T(8,128)(2,1)}, bf16[4,4,7,8,768]{4,3,2,1,0:T(8,128)(2,1)}, bf16[64,7,8,768]{3,2,1,0:T(8,128)(2,1)}) custom-call(s32[2]{0:T(128)} %pad_add_fusion.index_ref, bf16[4,4,4,7,8,768]{5,4,3,2,1,0:T(8,128)(2,1)} %bitcast.94, bf16[4,4,4,7,8,768]{5,4,3,2,1,0:T(8,128)(2,1)} %bitcast.15.refs_1_, ...), custom_call_target="tpu_custom_call", output_to_operand_aliasing={{2}: (7, {})} | custom-call | bytes 11000000 | tf_op jit(solution)/shard_map/pallas_call | solution.py:139
  215.2 11.4 %shard_map.465 = (f32[2,197,768]{2,1,0:T(8,128)}, bf16[2,197,768]{2,1,0:T(8,128)(2,1)}, bf16[64,8,768]{2,1,0:T(8,128)(2,1)}, bf16[64,8,768]{2,1,0:T(8,128)(2,1)}, f32[8,768]{1,0:T(8,128)}) custom-call(s32[1]{0:T(128)} %bitcast.core_ref, bf16[64,8,3200]{2,1,0:T(8,128)(2,1)} %bitcast.101, ...), custom_call_target="tpu_custom_call" | custom-call | flops 3227648000 | bytes 2000000000 | tf_op jit(solution)/shard_map/pallas_call | solution.py:501
  226.6 4.7 %collective-permute-done.7.refs_2_ = bf16[4,4,7,8,768]{4,3,2,1,0:T(8,128)(2,1)S(1)} collective-permute-done((bf16[4,4,7,8,768]{4,3,2,1,0:T(8,128)(2,1)}, bf16[4,4,7,8,768]{4,3,2,1,0:T(8,128)(2,1)S(1)}, u32[]{:S(2)}, u32[]{:S(2)}) %collective-permute-start.7) | collective-permute-done | bytes 1376288 | tf_op jit(solution)/shard_map/ppermute | solution.py:95
  234.2 7.5 %shard_map.466 = (bf16[4,4,7,8,768]{4,3,2,1,0:T(8,128)(2,1)}, bf16[4,4,7,8,768]{4,3,2,1,0:T(8,128)(2,1)}, bf16[4,4,7,8,768]{4,3,2,1,0:T(8,128)(2,1)}) custom-call(s32[3]{0:T(128)} %pad_add_fusion.1.index_ref, bf16[4,4,4,7,8,768]{5,4,3,2,1,0:T(8,128)(2,1)} %bitcast.95, bf16[4,4,4,7,8,768]{5,4,3,2,1,0:T(8,128)(2,1)} %bitcast.15.refs_1_, ...), custom_call_target="tpu_custom_call" | custom-call | bytes 16500000 | tf_op jit(solution)/shard_map/pallas_call | solution.py:139
  244.2 8.9 %shard_map.467.rest_0_.qkv_grad0_ref = bf16[197,2304]{1,0:T(8,128)(2,1)} custom-call(bf16[2,197,2304]{2,1,0:T(8,128)(2,1)} %get-tuple-element.95.qkv_ref, bf16[2,197,768]{2,1,0:T(8,128)(2,1)} %get-tuple-element.120.grad_ref, bf16[4,4,7,8,768]{4,3,2,1,0:T(8,128)(2,1)} %get-tuple-element.124.rest_0_, bf16[4,4,7,8,768]{4,3,2,1,0:T(8,128)(2,1)} %get-tuple-element.125.rest_1_, ...), custom_call_target="tpu_custom_call" | custom-call | flops 1613824000 | bytes 2000000000 | tf_op jit(solution)/shard_map/pallas_call | solution.py:501
  253.1 8.9 %shard_map.468.refs_9_.qkv_grad1_ref = bf16[197,2304]{1,0:T(8,128)(2,1)} custom-call(bf16[2,197,2304]{2,1,0:T(8,128)(2,1)} %get-tuple-element.95.qkv_ref, bf16[2,197,768]{2,1,0:T(8,128)(2,1)} %get-tuple-element.120.grad_ref, bf16[197,2304]{1,0:T(8,128)(2,1)} %shard_map.467.rest_0_.qkv_grad0_ref), custom_call_target="tpu_custom_call" | custom-call | flops 1613824000 | bytes 2000000000 | tf_op jit(solution)/shard_map/pallas_call | solution.py:501
  263.5 7.9 %shard_map.469 = (bf16[4,4,7,8,768]{4,3,2,1,0:T(8,128)(2,1)}, bf16[4,4,7,8,768]{4,3,2,1,0:T(8,128)(2,1)}, bf16[4,4,7,8,768]{4,3,2,1,0:T(8,128)(2,1)}) custom-call(s32[3]{0:T(128)} %pad_add_fusion.2.index_ref, bf16[4,4,4,7,8,768]{5,4,3,2,1,0:T(8,128)(2,1)} %bitcast.96, bf16[4,4,4,7,8,768]{5,4,3,2,1,0:T(8,128)(2,1)} %bitcast.15.refs_1_, ...), custom_call_target="tpu_custom_call" | custom-call | bytes 16500000 | tf_op jit(solution)/shard_map/pallas_call | solution.py:139
  277.5 17.2 %shard_map.471 = (bf16[64,8,2304]{2,1,0:T(8,128)(2,1)}, bf16[64,8,2304]{2,1,0:T(8,128)(2,1)}, bf16[64,8,128]{2,1,0:T(8,128)(2,1)}, bf16[64,8,128]{2,1,0:T(8,128)(2,1)}, f32[2,197,768]{2,1,0:T(8,128)}) custom-call(s32[1]{0:T(128)} %bitcast.core_ref, bf16[64,8,3200]{2,1,0:T(8,128)(2,1)} %bitcast.102, ...), custom_call_target="tpu_custom_call" | custom-call | flops 4034560000 | bytes 2000000000 | tf_op jit(solution)/shard_map/pallas_call | solution.py:501
  298.2 6.7 %collective-permute-done.13.refs_1_ = bf16[4,7,8,768]{3,2,1,0:T(8,128)(2,1)S(1)} collective-permute-done((bf16[4,7,8,768]{3,2,1,0:T(8,128)(2,1)S(1)}, bf16[4,7,8,768]{3,2,1,0:T(8,128)(2,1)S(1)}, u32[]{:S(2)}, u32[]{:S(2)}) %collective-permute-start.13) | collective-permute-done | bytes 344096 | tf_op jit(solution)/shard_map/ppermute | solution.py:95
  305.6 6.3 %shard_map.472 = (bf16[4,7,8,768]{3,2,1,0:T(8,128)(2,1)}, bf16[4,4,7,8,768]{4,3,2,1,0:T(8,128)(2,1)}, bf16[4,4,7,8,768]{4,3,2,1,0:T(8,128)(2,1)}) custom-call(s32[3]{0:T(128)} %pad_add_fusion.4.index_ref, bf16[4,4,7,8,768]{4,3,2,1,0:T(8,128)(2,1)} %get-tuple-element.135.refs_0_, bf16[4,7,8,768]{3,2,1,0:T(8,128)(2,1)} %copy-done.18, ...), custom_call_target="tpu_custom_call" | custom-call | bytes 16500000 | tf_op jit(solution)/shard_map/pallas_call | solution.py:139
  317.5 5.1 %shard_map.473 = bf16[64,8,3200]{2,1,0:T(8,128)(2,1)} custom-call(bf16[64,8,2304]{2,1,0:T(8,128)(2,1)} %get-tuple-element.143.own_qkv, bf16[64,8,2304]{2,1,0:T(8,128)(2,1)} %copy-done.2, bf16[64,8,768]{2,1,0:T(8,128)(2,1)} %get-tuple-element.145.own_out, bf16[64,8,768]{2,1,0:T(8,128)(2,1)} %copy-done.14, ...), custom_call_target="tpu_custom_call" | custom-call | bytes 2000000000 | tf_op jit(solution)/shard_map/pallas_call | solution.py:501
  322.6 9.1 %collective-permute-done.17.refs_5_ = bf16[4,4,7,8,768]{4,3,2,1,0:T(8,128)(2,1)} collective-permute-done((bf16[4,4,7,8,768]{4,3,2,1,0:T(8,128)(2,1)}, bf16[4,4,7,8,768]{4,3,2,1,0:T(8,128)(2,1)}, u32[]{:S(2)}, u32[]{:S(2)}) %collective-permute-start.17) | collective-permute-done | bytes 1376288 | tf_op jit(solution)/shard_map/ppermute | solution.py:95
  331.7 5.5 %shard_map.474 = (bf16[4,7,8,768]{3,2,1,0:T(8,128)(2,1)}, bf16[4,7,8,768]{3,2,1,0:T(8,128)(2,1)}, bf16[4,4,7,8,768]{4,3,2,1,0:T(8,128)(2,1)}, bf16[4,4,8,3200]{3,2,1,0:T(8,128)(2,1)}) custom-call(s32[4]{0:T(128)} %pad_add_fusion.7.index_ref, bf16[4,4,7,8,768]{4,3,2,1,0:T(8,128)(2,1)} %get-tuple-element.135.refs_0_, bf16[4,7,8,768]{3,2,1,0:T(8,128)(2,1)} %copy-done.17, ...), custom_call_target="tpu_custom_call" | custom-call | bytes 22000000 | tf_op jit(solution)/shard_map/pallas_call | solution.py:139
  339.2 7.6 %collective-permute-done.21.refs_1_ = bf16[4,7,8,768]{3,2,1,0:T(8,128)(2,1)S(1)} collective-permute-done((bf16[4,7,8,768]{3,2,1,0:T(8,128)(2,1)}, bf16[4,7,8,768]{3,2,1,0:T(8,128)(2,1)S(1)}, u32[]{:S(2)}, u32[]{:S(2)}) %collective-permute-start.21) | collective-permute-done | bytes 344096 | tf_op jit(solution)/shard_map/ppermute | solution.py:95
  352.0 4.9 %shard_map.475 = (bf16[4,7,8,768]{3,2,1,0:T(8,128)(2,1)}, bf16[4,7,8,768]{3,2,1,0:T(8,128)(2,1)}, bf16[4,7,8,768]{3,2,1,0:T(8,128)(2,1)}, bf16[4,4,8,3200]{3,2,1,0:T(8,128)(2,1)}) custom-call(s32[4]{0:T(128)} %pad_add_fusion.6.index_ref, bf16[4,4,7,8,768]{4,3,2,1,0:T(8,128)(2,1)} %get-tuple-element.135.refs_0_, bf16[4,7,8,768]{3,2,1,0:T(8,128)(2,1)} %copy-done.21, ...), custom_call_target="tpu_custom_call" | custom-call | bytes 22000000 | tf_op jit(solution)/shard_map/pallas_call | solution.py:139
  357.7 8.0 %collective-permute-done.24.refs_1_ = bf16[4,7,8,768]{3,2,1,0:T(8,128)(2,1)S(1)} collective-permute-done((bf16[4,7,8,768]{3,2,1,0:T(8,128)(2,1)}, bf16[4,7,8,768]{3,2,1,0:T(8,128)(2,1)S(1)}, u32[]{:S(2)}, u32[]{:S(2)}) %collective-permute-start.24) | collective-permute-done | bytes 344096 | tf_op jit(solution)/shard_map/ppermute | solution.py:95
  365.7 4.9 %collective-permute-done.26.refs_5_ = bf16[4,4,8,3200]{3,2,1,0:T(8,128)(2,1)S(1)} collective-permute-done((bf16[4,4,8,3200]{3,2,1,0:T(8,128)(2,1)}, bf16[4,4,8,3200]{3,2,1,0:T(8,128)(2,1)S(1)}, u32[]{:S(2)}, u32[]{:S(2)}) %collective-permute-start.26) | collective-permute-done | bytes 819232 | tf_op jit(solution)/shard_map/ppermute | solution.py:95
  371.6 4.6 %shard_map.476 = (bf16[4,7,8,768]{3,2,1,0:T(8,128)(2,1)}, bf16[4,7,8,768]{3,2,1,0:T(8,128)(2,1)}, bf16[4,4,8,3200]{3,2,1,0:T(8,128)(2,1)}) custom-call(s32[3]{0:T(128)} %pad_add_fusion.5.index_ref, bf16[4,4,7,8,768]{4,3,2,1,0:T(8,128)(2,1)} %get-tuple-element.140.rest_1_.refs_2_.refs_0_, bf16[4,7,8,768]{3,2,1,0:T(8,128)(2,1)} %copy-done.25, ...), custom_call_target="tpu_custom_call" | custom-call | bytes 16500000 | tf_op jit(solution)/shard_map/pallas_call | solution.py:139
  382.2 4.6 %all-to-all-done.1 = bf16[4,7,8,768]{3,2,1,0:T(8,128)(2,1)S(1)} async-done(((bf16[4,7,8,768]{3,2,1,0:T(8,128)(2,1)}), bf16[4,7,8,768]{3,2,1,0:T(8,128)(2,1)S(1)}, u32[]{:S(2)}, u32[]{:S(2)}) %all-to-all-start.1) | async-done | bytes 344096 | tf_op jit(solution)/shard_map/all_to_all | solution.py:109
  391.9 4.6 %shard_map.477 = (bf16[4,7,8,768]{3,2,1,0:T(8,128)(2,1)}, bf16[4,7,8,768]{3,2,1,0:T(8,128)(2,1)}, bf16[4,4,8,3200]{3,2,1,0:T(8,128)(2,1)}) custom-call(s32[3]{0:T(128)} %pad_add_fusion.3.index_ref, bf16[4,4,7,8,768]{4,3,2,1,0:T(8,128)(2,1)} %get-tuple-element.140.rest_1_.refs_2_.refs_0_, bf16[4,7,8,768]{3,2,1,0:T(8,128)(2,1)} %copy-done.19, ...), custom_call_target="tpu_custom_call" | custom-call | bytes 16500000 | tf_op jit(solution)/shard_map/pallas_call | solution.py:139
  396.6 4.2 all-to-all-start.2
  406.9 8.7 %collective-permute-done.30.refs_1_ = bf16[4,7,8,768]{3,2,1,0:T(8,128)(2,1)} collective-permute-done((bf16[4,7,8,768]{3,2,1,0:T(8,128)(2,1)}, bf16[4,7,8,768]{3,2,1,0:T(8,128)(2,1)}, u32[]{:S(2)}, u32[]{:S(2)}) %collective-permute-start.30) | collective-permute-done | bytes 344096 | tf_op jit(solution)/shard_map/ppermute | solution.py:95
  (238 shorter events, 103.1 us)
Async XLA Ops:
  7.2 127.6 %all-gather.3.cloned.1.call-start = ((), (), s32[]{:S(2)}) async-start(), calls=%async_computation.4 | async-start | bytes 33288192 | tf_op jit(solution)/shard_map/all_gather | solution.py:559
  14.8 23.5 %all-to-all-start = ((bf16[16,8,3200]{2,1,0:T(8,128)(2,1)}), bf16[16,8,3200]{2,1,0:T(8,128)(2,1)}, u32[]{:S(2)}, u32[]{:S(2)}) async-start(bf16[16,8,3200]{2,1,0:T(8,128)(2,1)} %broadcast_in_dim.38), calls=%async_computation | async-start | bytes 1638400 | tf_op jit(solution)/shard_map/all_to_all | solution.py:65
  38.3 14.8 %collective-permute-start = (bf16[16,8,3200]{2,1,0:T(8,128)(2,1)}, bf16[16,8,3200]{2,1,0:T(8,128)(2,1)S(1)}, u32[]{:S(2)}, u32[]{:S(2)}) collective-permute-start(bf16[16,8,3200]{2,1,0:T(8,128)(2,1)} %all-to-all-done), channel_id=1, source_target_pairs={{0,32},{32,64},{64,96},{96,0},{1,97},{33,1},{65,33},{97,65},{2,34}... | collective-permute-start | bytes 2457608 | tf_op jit(solution)/shard_map/ppermute | solution.py:71
  53.1 20.9 %collective-permute-start.1 = (bf16[16,8,3200]{2,1,0:T(8,128)(2,1)S(1)}, bf16[16,8,3200]{2,1,0:T(8,128)(2,1)S(1)}, u32[]{:S(2)}, u32[]{:S(2)}) collective-permute-start(bf16[16,8,3200]{2,1,0:T(8,128)(2,1)S(1)} %collective-permute-done), channel_id=1, source_target_pairs={{0,32},{32,64},{64,96},{96,0},{1,97},{33,1},{65,33},{97,65},{2,34}... | collective-permute-start | bytes 2457608 | tf_op jit(solution)/shard_map/ppermute | solution.py:71
  74.0 24.2 %collective-permute-start.2 = (bf16[16,8,3200]{2,1,0:T(8,128)(2,1)S(1)}, bf16[16,8,3200]{2,1,0:T(8,128)(2,1)S(1)}, u32[]{:S(2)}, u32[]{:S(2)}) collective-permute-start(bf16[16,8,3200]{2,1,0:T(8,128)(2,1)S(1)} %collective-permute-done.1), channel_id=1, source_target_pairs={{0,32},{32,64},{64,96},{96,0},{1,97},{33,1},{65,33},{97,65},{2,34}... | collective-permute-start | bytes 2457608 | tf_op jit(solution)/shard_map/ppermute | solution.py:71
  98.3 10.7 %collective-permute-start.3 = (bf16[64,8,3200]{2,1,0:T(8,128)(2,1)S(1)}, bf16[64,8,3200]{2,1,0:T(8,128)(2,1)}, u32[]{:S(2)}, u32[]{:S(2)}) collective-permute-start(bf16[64,8,3200]{2,1,0:T(8,128)(2,1)S(1)} %bitcast.97), channel_id=1, source_target_pairs={{0,1},{1,0},{2,3},{3,2},{4,5},{5,4},{6,7},{7,6},{8,9},{9,8},{10,11... | collective-permute-start | bytes 9830408 | tf_op jit(solution)/shard_map/ppermute | solution.py:51
  156.1 21.9 %collective-permute-start.4 = (bf16[64,7,8,768]{3,2,1,0:T(8,128)(2,1)}, bf16[64,7,8,768]{3,2,1,0:T(8,128)(2,1)}, u32[]{:S(2)}, u32[]{:S(2)}) collective-permute-start(bf16[64,7,8,768]{3,2,1,0:T(8,128)(2,1)} %get-tuple-element.105), channel_id=1, source_target_pairs={{0,1},{1,0},{2,3},{3,2},{4,5},{5,4},{6,7},{7,6},{8,9},{9,8},{10,11... | collective-permute-start | bytes 16515080 | tf_op jit(solution)/shard_map/ppermute | solution.py:51
  181.8 22.8 %collective-permute-start.6 = (bf16[64,7,8,768]{3,2,1,0:T(8,128)(2,1)}, bf16[64,7,8,768]{3,2,1,0:T(8,128)(2,1)}, u32[]{:S(2)}, u32[]{:S(2)}) collective-permute-start(bf16[64,7,8,768]{3,2,1,0:T(8,128)(2,1)} %get-tuple-element.116), channel_id=1, source_target_pairs={{0,1},{1,0},{2,3},{3,2},{4,5},{5,4},{6,7},{7,6},{8,9},{9,8},{10,11... | collective-permute-start | bytes 16515080 | tf_op jit(solution)/shard_map/ppermute | solution.py:51
  182.0 22.5 %collective-permute-start.5 = (bf16[4,4,7,8,768]{4,3,2,1,0:T(8,128)(2,1)}, bf16[4,4,7,8,768]{4,3,2,1,0:T(8,128)(2,1)S(1)}, u32[]{:S(2)}, u32[]{:S(2)}) collective-permute-start(bf16[4,4,7,8,768]{4,3,2,1,0:T(8,128)(2,1)} %get-tuple-element.108.rest_1_), channel_id=1, source_target_pairs={{0,32},{32,64},{64,96},{96,0},{1,97},{33,1},{65,33},{97,65},{2,34}... | collective-permute-start | bytes 4128776 | tf_op jit(solution)/shard_map/ppermute | solution.py:95
  211.3 21.7 %collective-permute-start.9 = (bf16[64,7,8,768]{3,2,1,0:T(8,128)(2,1)}, bf16[64,7,8,768]{3,2,1,0:T(8,128)(2,1)}, u32[]{:S(2)}, u32[]{:S(2)}) collective-permute-start(bf16[64,7,8,768]{3,2,1,0:T(8,128)(2,1)} %get-tuple-element.122), channel_id=1, source_target_pairs={{0,1},{1,0},{2,3},{3,2},{4,5},{5,4},{6,7},{7,6},{8,9},{9,8},{10,11... | collective-permute-start | bytes 16515080 | tf_op jit(solution)/shard_map/ppermute | solution.py:51
  211.6 19.7 %collective-permute-start.7 = (bf16[4,4,7,8,768]{4,3,2,1,0:T(8,128)(2,1)}, bf16[4,4,7,8,768]{4,3,2,1,0:T(8,128)(2,1)S(1)}, u32[]{:S(2)}, u32[]{:S(2)}) collective-permute-start(bf16[4,4,7,8,768]{4,3,2,1,0:T(8,128)(2,1)} %get-tuple-element.118.rest_0_), channel_id=1, source_target_pairs={{0,32},{32,64},{64,96},{96,0},{1,97},{33,1},{65,33},{97,65},{2,34}... | collective-permute-start | bytes 4128776 | tf_op jit(solution)/shard_map/ppermute | solution.py:95
  213.3 19.7 %collective-permute-start.8 = (bf16[4,4,7,8,768]{4,3,2,1,0:T(8,128)(2,1)}, bf16[4,4,7,8,768]{4,3,2,1,0:T(8,128)(2,1)S(1)}, u32[]{:S(2)}, u32[]{:S(2)}) collective-permute-start(bf16[4,4,7,8,768]{4,3,2,1,0:T(8,128)(2,1)} %get-tuple-element.119.rest_1_), channel_id=1, source_target_pairs={{0,8},{8,16},{16,24},{24,0},{1,25},{9,1},{17,9},{25,17},{2,10},{10... | collective-permute-start | bytes 4128776 | tf_op jit(solution)/shard_map/ppermute | solution.py:95
  241.6 20.4 %collective-permute-start.10 = (bf16[4,4,7,8,768]{4,3,2,1,0:T(8,128)(2,1)}, bf16[4,4,7,8,768]{4,3,2,1,0:T(8,128)(2,1)S(1)}, u32[]{:S(2)}, u32[]{:S(2)}) collective-permute-start(bf16[4,4,7,8,768]{4,3,2,1,0:T(8,128)(2,1)} %get-tuple-element.124.rest_0_), channel_id=1, source_target_pairs={{0,32},{32,64},{64,96},{96,0},{1,97},{33,1},{65,33},{97,65},{2,34}... | collective-permute-start | bytes 4128776 | tf_op jit(solution)/shard_map/ppermute | solution.py:95
  241.6 20.4 %collective-permute-start.11 = (bf16[4,4,7,8,768]{4,3,2,1,0:T(8,128)(2,1)}, bf16[4,4,7,8,768]{4,3,2,1,0:T(8,128)(2,1)S(1)}, u32[]{:S(2)}, u32[]{:S(2)}) collective-permute-start(bf16[4,4,7,8,768]{4,3,2,1,0:T(8,128)(2,1)} %get-tuple-element.125.rest_1_), channel_id=1, source_target_pairs={{0,8},{8,16},{16,24},{24,0},{1,25},{9,1},{17,9},{25,17},{2,10},{10... | collective-permute-start | bytes 4128776 | tf_op jit(solution)/shard_map/ppermute | solution.py:95
  242.2 19.9 %collective-permute-start.12 = (bf16[4,4,7,8,768]{4,3,2,1,0:T(8,128)(2,1)}, bf16[4,4,7,8,768]{4,3,2,1,0:T(8,128)(2,1)}, u32[]{:S(2)}, u32[]{:S(2)}) collective-permute-start(bf16[4,4,7,8,768]{4,3,2,1,0:T(8,128)(2,1)} %get-tuple-element.126.rest_2_), channel_id=1, source_target_pairs={{0,2},{2,4},{4,6},{6,0},{1,7},{3,1},{5,3},{7,5},{8,10},{10,12},{12... | collective-permute-start | bytes 4128776 | tf_op jit(solution)/shard_map/ppermute | solution.py:95
  271.4 33.4 %collective-permute-start.14 = (bf16[4,4,7,8,768]{4,3,2,1,0:T(8,128)(2,1)}, bf16[4,4,7,8,768]{4,3,2,1,0:T(8,128)(2,1)}, u32[]{:S(2)}, u32[]{:S(2)}) collective-permute-start(bf16[4,4,7,8,768]{4,3,2,1,0:T(8,128)(2,1)} %get-tuple-element.137), channel_id=1, source_target_pairs={{0,8},{8,16},{16,24},{24,0},{1,25},{9,1},{17,9},{25,17},{2,10},{10... | collective-permute-start | bytes 4128776 | tf_op jit(solution)/shard_map/ppermute | solution.py:95
  272.9 31.9 %collective-permute-start.15 = (bf16[4,4,7,8,768]{4,3,2,1,0:T(8,128)(2,1)}, bf16[4,4,7,8,768]{4,3,2,1,0:T(8,128)(2,1)}, u32[]{:S(2)}, u32[]{:S(2)}) collective-permute-start(bf16[4,4,7,8,768]{4,3,2,1,0:T(8,128)(2,1)} %get-tuple-element.138), channel_id=1, source_target_pairs={{0,2},{2,4},{4,6},{6,0},{1,7},{3,1},{5,3},{7,5},{8,10},{10,12},{12... | collective-permute-start | bytes 4128776 | tf_op jit(solution)/shard_map/ppermute | solution.py:95
  294.7 21.1 %collective-permute-start.18 = (bf16[64,8,2304]{2,1,0:T(8,128)(2,1)}, bf16[64,8,2304]{2,1,0:T(8,128)(2,1)S(1)}, u32[]{:S(2)}, u32[]{:S(2)}) collective-permute-start(bf16[64,8,2304]{2,1,0:T(8,128)(2,1)} %get-tuple-element.144), channel_id=1, source_target_pairs={{0,1},{1,0},{2,3},{3,2},{4,5},{5,4},{6,7},{7,6},{8,9},{9,8},{10,11... | collective-permute-start | bytes 7077896 | tf_op jit(solution)/shard_map/ppermute | solution.py:51
  311.9 19.8 %collective-permute-start.17 = (bf16[4,4,7,8,768]{4,3,2,1,0:T(8,128)(2,1)}, bf16[4,4,7,8,768]{4,3,2,1,0:T(8,128)(2,1)}, u32[]{:S(2)}, u32[]{:S(2)}) collective-permute-start(bf16[4,4,7,8,768]{4,3,2,1,0:T(8,128)(2,1)} %get-tuple-element.142.rest_2_), channel_id=1, source_target_pairs={{0,2},{2,4},{4,6},{6,0},{1,7},{3,1},{5,3},{7,5},{8,10},{10,12},{12... | collective-permute-start | bytes 4128776 | tf_op jit(solution)/shard_map/ppermute | solution.py:95
  313.1 9.5 %collective-permute-start.16 = (bf16[4,7,8,768]{3,2,1,0:T(8,128)(2,1)}, bf16[4,7,8,768]{3,2,1,0:T(8,128)(2,1)S(1)}, u32[]{:S(2)}, u32[]{:S(2)}) collective-permute-start(bf16[4,7,8,768]{3,2,1,0:T(8,128)(2,1)} %get-tuple-element.141.rest_0_), channel_id=1, source_target_pairs={{0,8},{8,16},{16,24},{24,0},{1,25},{9,1},{17,9},{25,17},{2,10},{10... | collective-permute-start | bytes 1032200 | tf_op jit(solution)/shard_map/ppermute | solution.py:95
  337.2 13.8 %collective-permute-start.23 = (bf16[4,4,8,3200]{3,2,1,0:T(8,128)(2,1)}, bf16[4,4,8,3200]{3,2,1,0:T(8,128)(2,1)S(1)}, u32[]{:S(2)}, u32[]{:S(2)}) collective-permute-start(bf16[4,4,8,3200]{3,2,1,0:T(8,128)(2,1)} %get-tuple-element.151), channel_id=1, source_target_pairs={{0,32},{32,64},{64,96},{96,0},{1,97},{33,1},{65,33},{97,65},{2,34}... | collective-permute-start | bytes 2457608 | tf_op jit(solution)/shard_map/ppermute | solution.py:95
  338.1 8.7 %collective-permute-start.21 = (bf16[4,7,8,768]{3,2,1,0:T(8,128)(2,1)}, bf16[4,7,8,768]{3,2,1,0:T(8,128)(2,1)S(1)}, u32[]{:S(2)}, u32[]{:S(2)}) collective-permute-start(bf16[4,7,8,768]{3,2,1,0:T(8,128)(2,1)} %get-tuple-element.148), channel_id=1, source_target_pairs={{0,8},{8,16},{16,24},{24,0},{1,25},{9,1},{17,9},{25,17},{2,10},{10... | collective-permute-start | bytes 1032200 | tf_op jit(solution)/shard_map/ppermute | solution.py:95
  338.6 8.7 %collective-permute-start.22 = (bf16[4,7,8,768]{3,2,1,0:T(8,128)(2,1)}, bf16[4,7,8,768]{3,2,1,0:T(8,128)(2,1)S(1)}, u32[]{:S(2)}, u32[]{:S(2)}) collective-permute-start(bf16[4,7,8,768]{3,2,1,0:T(8,128)(2,1)} %get-tuple-element.149), channel_id=1, source_target_pairs={{0,2},{2,4},{4,6},{6,0},{1,7},{3,1},{5,3},{7,5},{8,10},{10,12},{12... | collective-permute-start | bytes 1032200 | tf_op jit(solution)/shard_map/ppermute | solution.py:95
  356.9 13.8 %collective-permute-start.26 = (bf16[4,4,8,3200]{3,2,1,0:T(8,128)(2,1)}, bf16[4,4,8,3200]{3,2,1,0:T(8,128)(2,1)S(1)}, u32[]{:S(2)}, u32[]{:S(2)}) collective-permute-start(bf16[4,4,8,3200]{3,2,1,0:T(8,128)(2,1)} %get-tuple-element.154), channel_id=1, source_target_pairs={{0,32},{32,64},{64,96},{96,0},{1,97},{33,1},{65,33},{97,65},{2,34}... | collective-permute-start | bytes 2457608 | tf_op jit(solution)/shard_map/ppermute | solution.py:95
  356.9 8.7 %collective-permute-start.24 = (bf16[4,7,8,768]{3,2,1,0:T(8,128)(2,1)}, bf16[4,7,8,768]{3,2,1,0:T(8,128)(2,1)S(1)}, u32[]{:S(2)}, u32[]{:S(2)}) collective-permute-start(bf16[4,7,8,768]{3,2,1,0:T(8,128)(2,1)} %get-tuple-element.152), channel_id=1, source_target_pairs={{0,2},{2,4},{4,6},{6,0},{1,7},{3,1},{5,3},{7,5},{8,10},{10,12},{12... | collective-permute-start | bytes 1032200 | tf_op jit(solution)/shard_map/ppermute | solution.py:95
  357.0 8.7 %collective-permute-start.25 = (bf16[4,7,8,768]{3,2,1,0:T(8,128)(2,1)}, bf16[4,7,8,768]{3,2,1,0:T(8,128)(2,1)S(1)}, u32[]{:S(2)}, u32[]{:S(2)}) collective-permute-start(bf16[4,7,8,768]{3,2,1,0:T(8,128)(2,1)} %get-tuple-element.153), channel_id=1, source_target_pairs={{0,8},{8,16},{16,24},{24,0},{1,25},{9,1},{17,9},{25,17},{2,10},{10... | collective-permute-start | bytes 1032200 | tf_op jit(solution)/shard_map/ppermute | solution.py:95
  376.1 14.1 %collective-permute-start.29 = (bf16[4,4,8,3200]{3,2,1,0:T(8,128)(2,1)}, bf16[4,4,8,3200]{3,2,1,0:T(8,128)(2,1)S(1)}, u32[]{:S(2)}, u32[]{:S(2)}) collective-permute-start(bf16[4,4,8,3200]{3,2,1,0:T(8,128)(2,1)} %get-tuple-element.157), channel_id=1, source_target_pairs={{0,32},{32,64},{64,96},{96,0},{1,97},{33,1},{65,33},{97,65},{2,34}... | collective-permute-start | bytes 2457608 | tf_op jit(solution)/shard_map/ppermute | solution.py:95
  376.2 10.7 %all-to-all-start.1 = ((bf16[4,7,8,768]{3,2,1,0:T(8,128)(2,1)}), bf16[4,7,8,768]{3,2,1,0:T(8,128)(2,1)S(1)}, u32[]{:S(2)}, u32[]{:S(2)}) async-start(bf16[4,7,8,768]{3,2,1,0:T(8,128)(2,1)} %get-tuple-element.158), calls=%async_computation.1 | async-start | bytes 688128 | tf_op jit(solution)/shard_map/all_to_all | solution.py:109
  379.6 10.5 %collective-permute-start.27 = (bf16[4,7,8,768]{3,2,1,0:T(8,128)(2,1)}, bf16[4,7,8,768]{3,2,1,0:T(8,128)(2,1)S(1)}, u32[]{:S(2)}, u32[]{:S(2)}) collective-permute-start(bf16[4,7,8,768]{3,2,1,0:T(8,128)(2,1)} %get-tuple-element.155), channel_id=1, source_target_pairs={{0,2},{2,4},{4,6},{6,0},{1,7},{3,1},{5,3},{7,5},{8,10},{10,12},{12... | collective-permute-start | bytes 1032200 | tf_op jit(solution)/shard_map/ppermute | solution.py:95
  396.6 24.2 %all-to-all-start.2 = ((bf16[16,8,3200]{2,1,0:T(8,128)(2,1)}), bf16[16,8,3200]{2,1,0:T(8,128)(2,1)S(1)}, u32[]{:S(2)}, u32[]{:S(2)}) async-start(bf16[16,8,3200]{2,1,0:T(8,128)(2,1)} %bitcast.110), calls=%async_computation.2 | async-start | bytes 1638400 | tf_op jit(solution)/shard_map/all_to_all | solution.py:109
  400.9 14.8 %collective-permute-start.30 = (bf16[4,7,8,768]{3,2,1,0:T(8,128)(2,1)}, bf16[4,7,8,768]{3,2,1,0:T(8,128)(2,1)}, u32[]{:S(2)}, u32[]{:S(2)}) collective-permute-start(bf16[4,7,8,768]{3,2,1,0:T(8,128)(2,1)} %get-tuple-element.161), channel_id=1, source_target_pairs={{0,8},{8,16},{16,24},{24,0},{1,25},{9,1},{17,9},{25,17},{2,10},{10... | collective-permute-start | bytes 1032200 | tf_op jit(solution)/shard_map/ppermute | solution.py:95
  420.8 12.9 %all-to-all-start.3 = ((bf16[4,14,8,768]{3,2,1,0:T(8,128)(2,1)}), bf16[4,14,8,768]{3,2,1,0:T(8,128)(2,1)S(1)}, u32[]{:S(2)}, u32[]{:S(2)}) async-start(bf16[4,14,8,768]{3,2,1,0:T(8,128)(2,1)} %pad_maximum_fusion), calls=%async_computation.3 | async-start | bytes 1376256 | tf_op jit(solution)/shard_map/all_to_all | solution.py:109
  (53 other events, 331.9 us)
Sparse Core Ops, SparseCore 0:
  11.6 123.1 all-gather.2
